TPU v7x, 32 devices: a whole 2x2x4 slice. The times are simulated.
32 devices in a mesh: tm: 16 (over z, x, core), sec: 2 (over y).
Axes of the slice: x: 2, y: 2, z: 4, core: 2. Of those that a mesh axis runs over, the one named last changes fastest.
Arguments:
- record: float32 [768, 8192], P('sec', 'tm'), may hold values from -2000 to 2000
- fir_taps: float32 [65], replicated, may hold values from -0.75 to 0.75
- source_index: int32 [16], replicated, may hold values from 0 to 767
Outputs:
- xcorr: float32 [768, 16, 513], P(('sec', 'tm'))
All inputs are finite; a program needn't handle non-finite values.
Results may differ from a plain program's by a relative error of at most 0.004.
Values may be sent and summed in bfloat16 or wider, within the bound.
No kernel may reach another device: no remote copies, remote signals or barrier semaphores. Data moves between devices by JAX's collectives and lax.ppermute only.
A program may use at most 320 MiB of HBM per device.

v0:
```python
import math

import jax
import jax.numpy as jnp
from jax import lax
from jax.sharding import PartitionSpec as P

HALF_LAG = 256


eps = 1e-06
lag_group = 64
band_rows = 128


def padded(array, sides, width):
    for axis, dim in sides:
        count, length = (lax.axis_size(axis), array.shape[dim])
        up = [(i, (i + 1) % count) for i in range(count - 1)]
        down = [(j, i) for i, j in up]
        last = lax.slice_in_dim(array, length - width, length, axis=dim)
        leading = lax.slice_in_dim(array, 0, width, axis=dim)
        before = lax.ppermute(last, axis, up)
        after = lax.ppermute(leading, axis, down)
        array = jnp.concatenate([before, array, after], axis=dim)
    return array


def unit_rows(rows):
    energy = jnp.sqrt(jnp.mean(rows * rows, axis=1) + eps)
    return (rows / energy[:, None]).astype(jnp.bfloat16)


def correlate(pilots, units):
    nlag = 2 * HALF_LAG + 1
    shifts = -(-nlag // lag_group)
    samples = units.shape[1]
    count = units.shape[0]
    sources = pilots.shape[0]
    nblocks = samples // lag_group
    padded_len = (nblocks + shifts) * lag_group
    shifted = jnp.pad(units, ((0, 0), (HALF_LAG, padded_len - samples - HALF_LAG)))
    unit_blocks = shifted.reshape(count, nblocks + shifts, lag_group)
    paired = jnp.concatenate([unit_blocks[:, :-1], unit_blocks[:, 1:]], axis=2)
    pilot_blocks = pilots.reshape(sources, nblocks, lag_group)
    outputs = []
    for shift in range(shifts):
        window = paired[:, shift : shift + nblocks]
        grams = jnp.einsum(
            "sbi,cbj->scij", pilot_blocks, window, preferred_element_type=jnp.float32
        )
        flat = grams.reshape(sources, count, lag_group * 2 * lag_group)
        flat = jnp.pad(flat, ((0, 0), (0, 0), (0, lag_group)))
        skewed = flat.reshape(sources, count, lag_group, 2 * lag_group + 1)[:, :, :, :lag_group]
        outputs.append(jnp.sum(skewed, axis=2))
    result = jnp.concatenate(outputs, axis=2).transpose(1, 0, 2)[:, :, :nlag]
    return result * (1.0 / math.sqrt(samples))


def band_filter(haloed, fir_taps, section_rows):
    tap_count = fir_taps.shape[0]
    height = min(band_rows, section_rows)
    blocks = section_rows // height
    slab_len = haloed.shape[1]
    spare = (blocks + 1) * height - haloed.shape[0]
    extended = jnp.pad(haloed, ((0, spare), (0, 0))).reshape(blocks + 1, height, slab_len)
    out_idx = jnp.arange(height, dtype=jnp.int32)[:, None]
    in_idx = jnp.arange(height, dtype=jnp.int32)[None, :]
    tap_pos = jnp.arange(tap_count, dtype=jnp.int32)
    near_off = in_idx - out_idx
    far_off = in_idx + height - out_idx
    near_band = jnp.sum(
        jnp.where(near_off[:, :, None] == tap_pos[None, None, :], fir_taps[None, None, :], 0.0),
        axis=2,
    )
    far_band = jnp.sum(
        jnp.where(far_off[:, :, None] == tap_pos[None, None, :], fir_taps[None, None, :], 0.0),
        axis=2,
    )
    near_part = jnp.einsum("ij,bjt->bit", near_band, extended[:-1], precision=lax.Precision.HIGHEST)
    far_part = jnp.einsum("ij,bjt->bit", far_band, extended[1:], precision=lax.Precision.HIGHEST)
    return (near_part + far_part).reshape(section_rows, slab_len)


def shards(record, fir_taps, source_index):
    section_rows, slab_len = record.shape
    tap_count = fir_taps.shape[0]
    half_width = tap_count // 2
    time_devices = lax.axis_size("tm")
    haloed = padded(record, (("sec", 0),), half_width)
    filtered = band_filter(haloed, fir_taps, section_rows)
    channel_ids = lax.axis_index("sec") * section_rows + jnp.arange(section_rows, dtype=jnp.int32)
    selector = (source_index[:, None] == channel_ids[None, :]).astype(jnp.float32)
    local_traces = jnp.dot(selector, filtered, precision=lax.Precision.HIGHEST)
    summed = lax.psum(local_traces, "sec")
    traces = lax.all_gather(summed, "tm", axis=1, tiled=True)
    pilots = unit_rows(traces)
    stacked = filtered.reshape(time_devices, section_rows // time_devices, slab_len)
    return correlate(
        pilots, unit_rows(lax.all_to_all(stacked, "tm", split_axis=0, concat_axis=2, tiled=True)[0])
    )


def solution(mesh):
    in_specs = (P("sec", "tm"), P(), P())
    out_specs = P(("sec", "tm"), None, None)
    return jax.shard_map(shards, mesh=mesh, in_specs=in_specs, out_specs=out_specs, check_vma=False)
```

profile of v0, /device:TPU:0, one launch (start us, length us, event | category | flops | bytes accessed | tf_op | source)
XLA Modules:
  0.0 716.0 jit_solution(7854579135728088242)
XLA Ops:
  0.0 0.9 fusion.63
  0.9 4.9 collective-permute-start
  5.8 1.3 collective-permute-start.1
  7.1 1.6 select_reduce_fusion.1
  8.7 3.2 collective-permute-done.1
  11.9 1.4 pad_maximum_fusion.1
  13.3 0.8 fusion.46
  14.2 1.7 convolution_add_fusion
  15.9 5.9 all-to-all-start
  21.8 1.6 fusion.49
  23.4 6.9 psum.7
  30.3 23.9 %all_gather.3 = f32[16,8192]{1,0:T(8,128)S(1)} all-gather(f32[16,512]{1,0:T(8,128)S(1)} %psum.7), channel_id=1, replica_groups=mesh['tm'=16,'sec'=2] {'tm'}, dimensions={1}, use_global_device_ids=true | all-gather | bytes 557056 | tf_op jit(solution)/shard_map/all_gather | solution.py:96
  54.2 0.2 multiply_reduce_fusion.1
  54.5 0.5 reshape.121
  55.1 0.2 multiply_reduce_fusion
  55.5 0.6 reshape.119
  56.1 0.4 fusion.62
  56.5 6.5 convolution_bitcast_fusion
  62.9 6.4 convolution_bitcast_fusion.1
  69.3 6.5 convolution_bitcast_fusion.2
  75.8 6.4 convolution_bitcast_fusion.3
  82.2 6.5 convolution_bitcast_fusion.4
  88.7 6.6 convolution_bitcast_fusion.5
  95.3 6.4 convolution_bitcast_fusion.6
  101.7 6.4 convolution_bitcast_fusion.7
  108.0 6.3 convolution_bitcast_fusion.8
  114.4 14.0 %reshape.138 = f32[16,24,8192]{2,0,1:T(8,128)} reshape(f32[16,24,64,128]{3,2,0,1:T(8,128)} %convolution_bitcast_fusion) | data formatting | bytes 25165824 | tf_op jit(solution)/shard_map/reshape | solution.py:52
  128.4 10.4 %pad.46 = f32[16,24,8256]{2,0,1:T(8,128)} pad(f32[16,24,8192]{2,0,1:T(8,128)} %reshape.138, f32[]{:T(128)} %constant.8.clone.1), padding=0_0x0_0x0_64 | pad | bytes 25264132 | tf_op jit(solution)/shard_map/jit(_pad)/pad | solution.py:53
  138.7 34.7 %reshape.139 = f32[16,24,64,129]{3,2,0,1:T(8,128)} reshape(f32[16,24,8256]{2,0,1:T(8,128)} %pad.46) | data formatting | bytes 25362432 | tf_op jit(solution)/shard_map/reshape | solution.py:54
  173.4 8.1 %slice_reduce_fusion = f32[16,24,64]{2,0,1:T(8,128)} fusion(f32[16,24,64,129]{3,2,0,1:T(8,128)} %reshape.139), kind=kLoop, calls=%fused_computation | loop fusion | flops 1548288 | bytes 6389760 | tf_op jit(solution)/shard_map/reduce_sum | solution.py:55
  181.5 13.8 %reshape.136 = f32[16,24,8192]{2,0,1:T(8,128)} reshape(f32[16,24,64,128]{3,2,0,1:T(8,128)} %convolution_bitcast_fusion.1) | data formatting | bytes 25165824 | tf_op jit(solution)/shard_map/reshape | solution.py:52
  195.3 10.4 %pad.45 = f32[16,24,8256]{2,0,1:T(8,128)} pad(f32[16,24,8192]{2,0,1:T(8,128)} %reshape.136, f32[]{:T(128)} %constant.8.clone.1), padding=0_0x0_0x0_64 | pad | bytes 25264132 | tf_op jit(solution)/shard_map/jit(_pad)/pad | solution.py:53
  205.7 34.7 %reshape.137 = f32[16,24,64,129]{3,2,0,1:T(8,128)} reshape(f32[16,24,8256]{2,0,1:T(8,128)} %pad.45) | data formatting | bytes 25362432 | tf_op jit(solution)/shard_map/reshape | solution.py:54
  240.4 8.1 %slice_reduce_fusion.1 = f32[16,24,64]{2,0,1:T(8,128)} fusion(f32[16,24,64,129]{3,2,0,1:T(8,128)} %reshape.137), kind=kLoop, calls=%fused_computation.1 | loop fusion | flops 1548288 | bytes 6389760 | tf_op jit(solution)/shard_map/reduce_sum | solution.py:55
  248.5 13.8 %reshape.134 = f32[16,24,8192]{2,0,1:T(8,128)} reshape(f32[16,24,64,128]{3,2,0,1:T(8,128)} %convolution_bitcast_fusion.2) | data formatting | bytes 25165824 | tf_op jit(solution)/shard_map/reshape | solution.py:52
  262.2 10.4 %pad.44 = f32[16,24,8256]{2,0,1:T(8,128)} pad(f32[16,24,8192]{2,0,1:T(8,128)} %reshape.134, f32[]{:T(128)} %constant.8.clone.1), padding=0_0x0_0x0_64 | pad | bytes 25264132 | tf_op jit(solution)/shard_map/jit(_pad)/pad | solution.py:53
  272.6 35.1 %reshape.135 = f32[16,24,64,129]{3,2,0,1:T(8,128)} reshape(f32[16,24,8256]{2,0,1:T(8,128)} %pad.44) | data formatting | bytes 25362432 | tf_op jit(solution)/shard_map/reshape | solution.py:54
  307.7 8.1 %slice_reduce_fusion.2 = f32[16,24,64]{2,0,1:T(8,128)} fusion(f32[16,24,64,129]{3,2,0,1:T(8,128)} %reshape.135), kind=kLoop, calls=%fused_computation.2 | loop fusion | flops 1548288 | bytes 6389760 | tf_op jit(solution)/shard_map/reduce_sum | solution.py:55
  315.8 13.8 %reshape.132 = f32[16,24,8192]{2,0,1:T(8,128)} reshape(f32[16,24,64,128]{3,2,0,1:T(8,128)} %convolution_bitcast_fusion.3) | data formatting | bytes 25165824 | tf_op jit(solution)/shard_map/reshape | solution.py:52
  329.6 10.4 %pad.43 = f32[16,24,8256]{2,0,1:T(8,128)} pad(f32[16,24,8192]{2,0,1:T(8,128)} %reshape.132, f32[]{:T(128)} %constant.8.clone.1), padding=0_0x0_0x0_64 | pad | bytes 25264132 | tf_op jit(solution)/shard_map/jit(_pad)/pad | solution.py:53
  339.9 34.7 %reshape.133 = f32[16,24,64,129]{3,2,0,1:T(8,128)} reshape(f32[16,24,8256]{2,0,1:T(8,128)} %pad.43) | data formatting | bytes 25362432 | tf_op jit(solution)/shard_map/reshape | solution.py:54
  374.6 7.4 %slice_reduce_fusion.3 = f32[16,24,64]{2,0,1:T(8,128)S(1)} fusion(f32[16,24,64,129]{3,2,0,1:T(8,128)} %reshape.133), kind=kLoop, calls=%fused_computation.3 | loop fusion | flops 1548288 | bytes 6389760 | tf_op jit(solution)/shard_map/reduce_sum | solution.py:55
  382.1 13.8 %reshape.130 = f32[16,24,8192]{2,0,1:T(8,128)} reshape(f32[16,24,64,128]{3,2,0,1:T(8,128)} %convolution_bitcast_fusion.4) | data formatting | bytes 25165824 | tf_op jit(solution)/shard_map/reshape | solution.py:52
  395.8 10.4 %pad.42 = f32[16,24,8256]{2,0,1:T(8,128)} pad(f32[16,24,8192]{2,0,1:T(8,128)} %reshape.130, f32[]{:T(128)} %constant.8.clone.1), padding=0_0x0_0x0_64 | pad | bytes 25264132 | tf_op jit(solution)/shard_map/jit(_pad)/pad | solution.py:53
  406.2 34.8 %reshape.131 = f32[16,24,64,129]{3,2,0,1:T(8,128)} reshape(f32[16,24,8256]{2,0,1:T(8,128)} %pad.42) | data formatting | bytes 25362432 | tf_op jit(solution)/shard_map/reshape | solution.py:54
  441.0 7.4 %slice_reduce_fusion.4 = f32[16,24,64]{2,0,1:T(8,128)S(1)} fusion(f32[16,24,64,129]{3,2,0,1:T(8,128)} %reshape.131), kind=kLoop, calls=%fused_computation.4 | loop fusion | flops 1548288 | bytes 6389760 | tf_op jit(solution)/shard_map/reduce_sum | solution.py:55
  448.5 13.8 %reshape.128 = f32[16,24,8192]{2,0,1:T(8,128)} reshape(f32[16,24,64,128]{3,2,0,1:T(8,128)} %convolution_bitcast_fusion.5) | data formatting | bytes 25165824 | tf_op jit(solution)/shard_map/reshape | solution.py:52
  462.3 10.4 %pad.41 = f32[16,24,8256]{2,0,1:T(8,128)} pad(f32[16,24,8192]{2,0,1:T(8,128)} %reshape.128, f32[]{:T(128)} %constant.8.clone.1), padding=0_0x0_0x0_64 | pad | bytes 25264132 | tf_op jit(solution)/shard_map/jit(_pad)/pad | solution.py:53
  472.6 34.7 %reshape.129 = f32[16,24,64,129]{3,2,0,1:T(8,128)} reshape(f32[16,24,8256]{2,0,1:T(8,128)} %pad.41) | data formatting | bytes 25362432 | tf_op jit(solution)/shard_map/reshape | solution.py:54
  507.3 7.4 %slice_reduce_fusion.5 = f32[16,24,64]{2,0,1:T(8,128)S(1)} fusion(f32[16,24,64,129]{3,2,0,1:T(8,128)} %reshape.129), kind=kLoop, calls=%fused_computation.5 | loop fusion | flops 1548288 | bytes 6389760 | tf_op jit(solution)/shard_map/reduce_sum | solution.py:55
  514.8 13.8 %reshape.126 = f32[16,24,8192]{2,0,1:T(8,128)} reshape(f32[16,24,64,128]{3,2,0,1:T(8,128)} %convolution_bitcast_fusion.6) | data formatting | bytes 25165824 | tf_op jit(solution)/shard_map/reshape | solution.py:52
  528.5 10.4 %pad.40 = f32[16,24,8256]{2,0,1:T(8,128)} pad(f32[16,24,8192]{2,0,1:T(8,128)} %reshape.126, f32[]{:T(128)} %constant.8.clone.1), padding=0_0x0_0x0_64 | pad | bytes 25264132 | tf_op jit(solution)/shard_map/jit(_pad)/pad | solution.py:53
  538.9 34.9 %reshape.127 = f32[16,24,64,129]{3,2,0,1:T(8,128)} reshape(f32[16,24,8256]{2,0,1:T(8,128)} %pad.40) | data formatting | bytes 25362432 | tf_op jit(solution)/shard_map/reshape | solution.py:54
  573.8 7.4 %slice_reduce_fusion.6 = f32[16,24,64]{2,0,1:T(8,128)S(1)} fusion(f32[16,24,64,129]{3,2,0,1:T(8,128)} %reshape.127), kind=kLoop, calls=%fused_computation.6 | loop fusion | flops 1548288 | bytes 6389760 | tf_op jit(solution)/shard_map/reduce_sum | solution.py:55
  581.2 13.8 %reshape.124 = f32[16,24,8192]{2,0,1:T(8,128)} reshape(f32[16,24,64,128]{3,2,0,1:T(8,128)} %convolution_bitcast_fusion.7) | data formatting | bytes 25165824 | tf_op jit(solution)/shard_map/reshape | solution.py:52
  595.0 10.4 %pad.39 = f32[16,24,8256]{2,0,1:T(8,128)} pad(f32[16,24,8192]{2,0,1:T(8,128)} %reshape.124, f32[]{:T(128)} %constant.8.clone.1), padding=0_0x0_0x0_64 | pad | bytes 25264132 | tf_op jit(solution)/shard_map/jit(_pad)/pad | solution.py:53
  605.4 34.7 %reshape.125 = f32[16,24,64,129]{3,2,0,1:T(8,128)} reshape(f32[16,24,8256]{2,0,1:T(8,128)} %pad.39) | data formatting | bytes 25362432 | tf_op jit(solution)/shard_map/reshape | solution.py:54
  640.1 7.4 %slice_reduce_fusion.7 = f32[16,24,64]{2,0,1:T(8,128)S(1)} fusion(f32[16,24,64,129]{3,2,0,1:T(8,128)} %reshape.125), kind=kLoop, calls=%fused_computation.7 | loop fusion | flops 1548288 | bytes 6389760 | tf_op jit(solution)/shard_map/reduce_sum | solution.py:55
  647.5 13.8 %reshape.122 = f32[16,24,8192]{2,0,1:T(8,128)} reshape(f32[16,24,64,128]{3,2,0,1:T(8,128)} %convolution_bitcast_fusion.8) | data formatting | bytes 25165824 | tf_op jit(solution)/shard_map/reshape | solution.py:52
  661.3 10.4 %pad.38 = f32[16,24,8256]{2,0,1:T(8,128)} pad(f32[16,24,8192]{2,0,1:T(8,128)} %reshape.122, f32[]{:T(128)} %constant.8.clone.1), padding=0_0x0_0x0_64 | pad | bytes 25264132 | tf_op jit(solution)/shard_map/jit(_pad)/pad | solution.py:53
  671.6 34.9 %reshape.123 = f32[16,24,64,129]{3,2,0,1:T(8,128)} reshape(f32[16,24,8256]{2,0,1:T(8,128)} %pad.38) | data formatting | bytes 25362432 | tf_op jit(solution)/shard_map/reshape | solution.py:54
  706.6 7.5 %slice_reduce_fusion.8 = f32[16,24,64]{2,0,1:T(8,128)S(1)} fusion(f32[16,24,64,129]{3,2,0,1:T(8,128)} %reshape.123), kind=kLoop, calls=%fused_computation.8 | loop fusion | flops 1548288 | bytes 6389760 | tf_op jit(solution)/shard_map/reduce_sum | solution.py:55
  714.1 0.6 concatenate.15
  714.7 1.0 slice_multiply_fusion
  (17 shorter events, 0.4 us)
Async XLA Ops:
  0.9 7.8 %collective-permute-start = (f32[32,512]{1,0:T(8,128)S(1)}, f32[32,512]{1,0:T(8,128)S(1)}, u32[]{:S(2)}, u32[]{:S(2)}) collective-permute-start(f32[32,512]{1,0:T(8,128)S(1)} %get-tuple-element.11), channel_id=1, source_target_pairs={{0,1},{2,3},{4,5},{6,7},{8,9},{10,11},{12,13},{14,15},{16,17},{18,... | collective-permute-start | bytes 196616 | tf_op jit(solution)/shard_map/ppermute | solution.py:23
  5.8 6.2 collective-permute-start.1
  15.9 39.1 %all-to-all-start = ((f32[16,24,512]{2,1,0:T(8,128)}), f32[16,24,512]{2,1,0:T(8,128)S(1)}, u32[]{:S(2)}, u32[]{:S(2)}) async-start(f32[16,24,512]{2,1,0:T(8,128)} %bitcast.5), calls=%async_computation | async-start | bytes 1572864 | tf_op jit(solution)/shard_map/all_to_all | solution.py:100
  706.6 7.5 %copy-start = (f32[16,24,64]{2,0,1:T(8,128)S(1)}, f32[16,24,64]{2,0,1:T(8,128)}, u32[]{:S(2)}) copy-start(f32[16,24,64]{2,0,1:T(8,128)} %slice_reduce_fusion) | copy-start | bytes 294916
  706.6 7.5 %copy-start.1 = (f32[16,24,64]{2,0,1:T(8,128)S(1)}, f32[16,24,64]{2,0,1:T(8,128)}, u32[]{:S(2)}) copy-start(f32[16,24,64]{2,0,1:T(8,128)} %slice_reduce_fusion.1) | copy-start | bytes 294916
  706.6 7.5 %copy-start.2 = (f32[16,24,64]{2,0,1:T(8,128)S(1)}, f32[16,24,64]{2,0,1:T(8,128)}, u32[]{:S(2)}) copy-start(f32[16,24,64]{2,0,1:T(8,128)} %slice_reduce_fusion.2) | copy-start | bytes 294916
where the time goes:
time: 723 us; the launch traced here: 716 us
  local copies, waits for them, and re-layouts  534 us (74%)
  other arithmetic  73.6 us (10%)
  matrix products  62 us (9%)
  blocking collectives  30.8 us (4%)
  starting transfers between devices  12.1 us (2%)
    reshape x9, local copies, waits for them, and re-layouts, correlate(): flat.reshape(sources, count, lag_group, 2 * lag_group + 1)  313 us
    reshape x9, local copies, waits for them, and re-layouts, correlate(): flat = grams.reshape(sources, count, lag_group * 2 * lag_group)  124 us
    pad x9, local copies, waits for them, and re-layouts, correlate(): flat = jnp.pad(flat, ((0, 0), (0, 0), (0, lag_group)))  93.3 us
    reduce_sum x9, other arithmetic, correlate(): outputs.append(jnp.sum(skewed, axis=2))  68.9 us
    dot_general x9, matrix products, correlate(): jnp.einsum('sbi,cbj->scij', pilot_blocks, window, preferred_element_type=...  57.9 us
    all_gather x1, blocking collectives, shards(): traces = lax.all_gather(summed, 'tm', axis=1, tiled=True)  23.9 us
  transfers between devices with their start and end apart: 3, of which 1 were waited for; matrix products, arithmetic and copies ran while one was open for 1% of the time, Pallas kernels for 0%

commit v1 on v0

v1 whole, which is shorter than its diff:
```python
import functools
import math

import jax
import jax.numpy as jnp
from jax import lax
from jax.experimental import pallas as pl
from jax.experimental.pallas import tpu as pltpu
from jax.sharding import PartitionSpec as P

f32 = jnp.float32
bf16 = jnp.bfloat16
HALF_LAG = 256
NLAG = 2 * HALF_LAG + 1
SCALE = 2.0**32
EPS = 1e-6 * SCALE * SCALE
G = 32
HALO = 32
SMEM = pltpu.SMEM
VMEM = pltpu.VMEM


def filter_kernel(index_ref, taps_ref, rec_ref, filt_ref, exch_ref, hi_ref, lo_ref, ext_ref, *, pair):
    rows, width = rec_ref.shape
    taps = taps_ref.shape[0]
    sources = index_ref.shape[0]
    lane = lax.broadcasted_iota(jnp.int32, (8, 256), 1)
    base = jnp.zeros((8, 256), f32)
    for m in range(taps):
        base = jnp.where(lane == m, taps_ref[m] * SCALE, base)
    tall = jnp.concatenate([base] * 16, axis=0)
    band = pltpu.roll(tall, 0, 1, stride=1, stride_axis=0)
    band_hi = band.astype(bf16)
    band_lo = (band - band_hi.astype(f32)).astype(bf16)
    both = jnp.concatenate([band_hi, band_lo], axis=0)
    edge = jnp.zeros((64, width), bf16)
    tiles = -(-(rows + 64) // 128)
    spare = hi_ref.shape[0] - 64 - rows
    for ref in (hi_ref, lo_ref):
        ref[:64, :] = edge
        ref[64 + rows :, :] = jnp.zeros((spare, width), bf16)
    rec = rec_ref[...]
    rec_hi = rec.astype(bf16)
    hi_ref[64 : 64 + rows, :] = rec_hi
    lo_ref[64 : 64 + rows, :] = (rec - rec_hi.astype(f32)).astype(bf16)
    for i in range(tiles):
        hi = hi_ref[128 * i : 128 * i + 256, :]
        lo = lo_ref[128 * i : 128 * i + 256, :]
        big = jnp.dot(both, hi, preferred_element_type=f32)
        small = jnp.dot(band_hi, lo, preferred_element_type=f32)
        ext_ref[128 * i : 128 * i + 128, :] = big[:128] + (big[128:] + small)
    filt_ref[...] = ext_ref[HALO : HALO + rows, :]
    first = lax.axis_index("sec") * rows - HALO
    for s in range(sources):
        row = index_ref[s] - first
        inside = jnp.logical_and(row >= 0, row < rows + 2 * HALO)
        at = jnp.where(inside, row, 0)
        exch_ref[s : s + 1, :] = jnp.where(inside, ext_ref[pl.ds(at, 1), :], 0.0)
    down = ext_ref[:HALO, :]
    up = ext_ref[HALO + rows : 2 * HALO + rows, :]
    if pair:
        exch_ref[sources:, :] = jnp.where(lax.axis_index("sec") == 0, up, down)
    else:
        exch_ref[sources : sources + HALO, :] = down
        exch_ref[sources + HALO :, :] = up


def filter_rows(record, fir_taps, source_index, pair):
    rows, width = record.shape
    sources = source_index.shape[0]
    tiles = -(-(rows + 64) // 128)
    deep = 128 * (tiles + 1)
    return pl.pallas_call(
        functools.partial(filter_kernel, pair=pair),
        out_shape=(
            jax.ShapeDtypeStruct((rows, width), f32),
            jax.ShapeDtypeStruct((sources + HALO * (1 if pair else 2), width), f32),
        ),
        in_specs=[
            pl.BlockSpec(memory_space=SMEM),
            pl.BlockSpec(memory_space=SMEM),
            pl.BlockSpec(memory_space=VMEM),
        ],
        scratch_shapes=[
            pltpu.VMEM((deep, width), bf16),
            pltpu.VMEM((deep, width), bf16),
            pltpu.VMEM((128 * tiles, width), f32),
        ],
        compiler_params=pltpu.CompilerParams(vmem_limit_bytes=24 * 1024 * 1024),
    )(source_index, fir_taps, record)


def pack_kernel(filt_ref, pilots_ref, low_ref, high_ref, out_ref, *, count):
    rows = filt_ref.shape[0]
    pilots = pilots_ref[...].astype(bf16)
    sources = pilots.shape[0]
    for d in range(out_ref.shape[0]):
        out_ref[d, :sources, :] = pilots
        lo, hi = d * count, (d + 1) * count
        part = filt_ref[lo:hi, :]
        if lo < HALO:
            n = min(hi, HALO) - lo
            add = low_ref[lo : lo + n, :]
            part = jnp.concatenate([part[:n] + add, part[n:]], axis=0) if n < count else part + add
        if hi > rows - HALO:
            n = hi - max(lo, rows - HALO)
            add = high_ref[max(lo, rows - HALO) - (rows - HALO) : hi - (rows - HALO), :]
            part = jnp.concatenate([part[: count - n], part[count - n :] + add], axis=0) if n < count else part + add
        out_ref[d, sources:, :] = part.astype(bf16)


def pack(filt, pilots, low, high, devices):
    rows, width = filt.shape
    count = rows // devices
    return pl.pallas_call(
        functools.partial(pack_kernel, count=count),
        out_shape=jax.ShapeDtypeStruct((devices, pilots.shape[0] + count, width), bf16),
        compiler_params=pltpu.CompilerParams(vmem_limit_bytes=24 * 1024 * 1024),
    )(filt, pilots, low, high)


def corr_kernel(x_ref, o_ref, p_ref, z_ref, acc_ref, os_ref, *, kc, count):
    wins, _, win = x_ref.shape
    T=wins*win
    p_ref[:, :128]=jnp.zeros((16,128),p_ref.dtype)
    p_ref[:, 128+T:]=jnp.zeros((16,p_ref.shape[1]-128-T),p_ref.dtype)
    esum=jnp.zeros((16,128),f32)
    usum=jnp.zeros((count,128),f32)
    for w in range(wins):
        pw=x_ref[w,0:16,:]
        p_ref[:,128+w*win:128+(w+1)*win]=pw.astype(p_ref.dtype)
        uw=x_ref[w,16:16+count,:].astype(f32)
        pf=pw.astype(f32)
        for q in range(win//128):
            s=slice(q*128,(q+1)*128)
            esum=esum+pf[:,s]*pf[:,s]; usum=usum+uw[:,s]*uw[:,s]
    nz=z_ref.shape[0]//128
    zero=jnp.zeros((count,128),f32)
    def utile(k):
        k=k-2
        if k<0 or k>=T//128: return zero
        w,q=divmod(k*128,win)
        return x_ref[w,16:16+count,q:q+128].astype(f32)
    lane=lax.broadcasted_iota(jnp.int32,(count,128),1)
    padrows=jnp.zeros((32-count,128),f32)
    rolled=None
    for k in range(nz+1):
        t=utile(k)
        nxt=[t]+[pltpu.roll(t,128-32*r,1) for r in (1,2,3)]
        if rolled is not None:
            parts=[]
            for r in range(4):
                v=rolled[r] if r==0 else jnp.where(lane<128-32*r, rolled[r], nxt[r])
                parts+= [v,padrows]
            blk=jnp.concatenate(parts,axis=0)
            z_ref[(k-1)*128:k*128,:]=blk.T.astype(bf16)
        rolled=nxt
    acc_ref[...]=jnp.zeros_like(acc_ref)
    steps=-(-(T+G)//kc)
    def body(i,_):
        t0=pl.multiple_of(i*kc,kc)
        X=p_ref[:,pl.ds(t0,kc+128)]
        rows=[]
        for j in range(G+1):
            rows.append((pltpu.roll(X,j,1) if j else X)[:,128:].astype(bf16))
        plate=jnp.concatenate(rows,axis=0)
        rhs=jnp.concatenate([z_ref[pl.ds(pl.multiple_of(t0+128*a,128),kc),:] for a in range(4)],axis=1)
        d=jnp.dot(plate,rhs,preferred_element_type=f32)
        for a in range(4): acc_ref[a]+=d[:,128*a:128*a+128]
        return 0
    lax.fori_loop(0,steps,body,0)
    es=lax.rsqrt(jnp.sum(esum,axis=1,keepdims=True)/T+EPS)
    ue=lax.rsqrt(jnp.sum(usum,axis=1,keepdims=True)/T+EPS)/math.sqrt(T)
    lane=lax.broadcasted_iota(jnp.int32,(count,128),1)
    for quad in range(4):
        scl=[jnp.broadcast_to(ue*jnp.broadcast_to(es[4*quad+m:4*quad+m+1],(count,1)),(count,128)) for m in range(4)]
        for a in range(4):
            blk=jnp.concatenate([acc_ref[a,pl.ds(4*quad+m,32,stride=16),:] for m in range(4)],axis=0)
            Y=blk.T
            for m in range(4):
                o=None
                for r in range(4):
                    v=Y[32*r:32*r+count,:]
                    sh=(32*(r-m))%128
                    v=pltpu.roll(v,sh,1) if sh else v
                    o=v if o is None else jnp.where(lane<32*r,o,v)
                os_ref[a,pl.ds(4*quad+m,count,stride=16),:]=o*scl[m]
    last=acc_ref[3,512:528,:]
    last=pltpu.roll(last,32,1)
    last=jnp.concatenate([last*es]+[jnp.zeros((112,128),f32)],axis=0).T[:count]*ue
    for s in range(16):
        v=pltpu.roll(last,(128-s)%128,1) if s else last
        os_ref[4,pl.ds(s,count,stride=16),:]=v
    for a in range(4): o_ref[:,128*a:128*a+128]=os_ref[a]
    o_ref[:,512:513]=os_ref[4][:,0:1]

def correlate(x):
    wins, rows, win = x.shape
    count = rows - 16
    samples = wins * win
    kc = 1664
    steps = -(-(samples + G) // kc)
    out = pl.pallas_call(
        functools.partial(corr_kernel, kc=kc, count=count),
        out_shape=jax.ShapeDtypeStruct((count * 16, NLAG), f32),
        scratch_shapes=[
            pltpu.VMEM((16, steps * kc + 128), bf16),
            pltpu.VMEM((steps * kc + 384, 128), bf16),
            pltpu.VMEM((4, (G + 1) * 16, 128), f32),
            pltpu.VMEM((5, count * 16, 128), f32),
        ],
        compiler_params=pltpu.CompilerParams(vmem_limit_bytes=48 * 1024 * 1024),
    )(x)
    return out.reshape(count, 16, NLAG)


def shards(record, fir_taps, source_index):
    sections = lax.axis_size("sec")
    pair = sections == 2
    sources = source_index.shape[0]
    filt, exch = filter_rows(record, fir_taps, source_index, pair)
    if pair:
        other = lax.ppermute(exch, "sec", [(0, 1), (1, 0)])
        pilots = exch[:sources] + other[:sources]
        here = lax.axis_index("sec")
        edge = other[sources:]
        low = jnp.where(here == 1, edge, 0.0)
        high = jnp.where(here == 0, edge, 0.0)
    else:
        pilots = lax.psum(exch[:sources], "sec")
        up = [(i, i + 1) for i in range(sections - 1)]
        down = [(i + 1, i) for i in range(sections - 1)]
        high = lax.ppermute(exch[sources : sources + HALO], "sec", down)
        low = lax.ppermute(exch[sources + HALO :], "sec", up)
    blocks = pack(filt, pilots, low, high, lax.axis_size("tm"))
    return correlate(lax.all_to_all(blocks, "tm", 0, 0, tiled=True))


def solution(mesh):
    in_specs = (P("sec", "tm"), P(), P())
    out_specs = P(("sec", "tm"), None, None)
    return jax.shard_map(shards, mesh=mesh, in_specs=in_specs, out_specs=out_specs, check_vma=False)
```

time: 723 us -> 43.9 us (0.06)
  local copies, waits for them, and re-layouts: 534 us -> 2.44 us
  other arithmetic: 73.6 us -> 0.02 us
  matrix products: 62 us -> 0 us
  Pallas kernels: 0 us -> 11.1 us
  starting transfers between devices: 12.1 us -> 3.03 us
    reshape x20 -> x0, local copies, waits for them, and re-layouts: 438 us -> none  [the longest x9 313 us: correlate(): flat.reshape(sources, count, lag_group, 2 * lag_group + 1)]
    pad x10 -> x0, local copies, waits for them, and re-layouts: 93.3 us -> none  [the longest x9 93.3 us: correlate(): flat = jnp.pad(flat, ((0, 0), (0, 0), (0, lag_group)))]
    reduce_sum x12 -> x0, other arithmetic: 70.9 us -> none  [the longest x9 68.9 us: correlate(): outputs.append(jnp.sum(skewed, axis=2))]
    dot_general x12 -> x0, matrix products: 62 us -> none  [the longest x9 57.9 us: correlate(): jnp.einsum('sbi,cbj->scij', pilot_blocks, window, preferred_element_type=...]
    all_to_all x0 -> x1, blocking collectives: none -> 24.3 us  [shards(): return correlate(lax.all_to_all(blocks, 'tm', 0, 0, tiled=True))]
    all_gather x1 -> x0, blocking collectives: 23.9 us -> none  [shards(): traces = lax.all_gather(summed, 'tm', axis=1, tiled=True)]
    pallas_call x0 -> x3, Pallas kernels: none -> 11.1 us  [the longest x1 9.86 us: correlate(): pl.pallas_call(functools.partial(corr_kernel, kc=kc, count=count), out_sh...]
  transfers between devices with their start and end apart: 3 -> 1, of which waited for: 1 -> 1; matrix products, arithmetic and copies ran while one was open for 1% -> 0% of each run, Pallas kernels for 0% -> 0%
where the time goes in v1:
time: 43.9 us; the launch traced here: 43.7 us
  blocking collectives  24.3 us (55%)
  Pallas kernels  11.1 us (25%)
  starting transfers between devices  3.03 us (7%)
  waiting for transfers between devices  2.79 us (6%)
  local copies, waits for them, and re-layouts  2.44 us (6%)
    all_to_all x1, blocking collectives, shards(): return correlate(lax.all_to_all(blocks, 'tm', 0, 0, tiled=True))  24.3 us
    pallas_call x1, Pallas kernels, correlate(): pl.pallas_call(functools.partial(corr_kernel, kc=kc, count=count), out_sh...  9.86 us
    ppermute x1, starting transfers between devices, shards(): other = lax.ppermute(exch, 'sec', [(0, 1), (1, 0)])  3.03 us
    ppermute x1, waiting for transfers between devices, shards(): other = lax.ppermute(exch, 'sec', [(0, 1), (1, 0)])  2.79 us
    unnamed x6, local copies, waits for them, and re-layouts  2.44 us
    pallas_call x1, Pallas kernels, filter_rows(): pl.pallas_call(functools.partial(filter_kernel, pair=pair), out_shape=(ja...  1.22 us
  transfers between devices with their start and end apart: 1, of which 1 were waited for; matrix products, arithmetic and copies ran while one was open for 0% of the time, Pallas kernels for 0%

profile of v1, /device:TPU:0, one launch (start us, length us, event | category | flops | bytes accessed | tf_op | source)
XLA Modules:
  0.0 43.7 jit_solution(1116453253140097629)
XLA Ops:
  0.0 0.0 copy-start
  0.0 1.1 %copy-done = f32[384,512]{1,0:T(8,128)S(1)} copy-done((f32[384,512]{1,0:T(8,128)S(1)}, f32[384,512]{1,0:T(8,128)}, u32[]{:S(2)}) %copy-start) | copy-done | bytes 786456
  1.1 0.0 copy-start.1
  1.1 0.7 %copy-done.1 = s32[16]{0:T(128)S(1)} copy-done((s32[16]{0:T(128)S(1)}, s32[16]{0:T(128)}, u32[]{:S(2)}) %copy-start.1) | copy-done | bytes 88
  1.8 0.0 copy-start.2
  1.8 0.7 %copy-done.2 = f32[65]{0:T(128)S(1)} copy-done((f32[65]{0:T(128)S(1)}, f32[65]{0:T(128)}, u32[]{:S(2)}) %copy-start.2) | copy-done | bytes 284
  2.4 1.2 %shard_map.37 = (f32[384,512]{1,0:T(8,128)S(1)}, f32[48,512]{1,0:T(8,128)S(1)}) custom-call(s32[16]{0:T(128)S(1)} %copy-done.1, f32[65]{0:T(128)S(1)} %copy-done.2, f32[384,512]{1,0:T(8,128)S(1)} %copy-done), custom_call_target="tpu_custom_call" | custom-call | tf_op jit(solution)/shard_map/pallas_call | solution.py:73
  3.7 3.0 %collective-permute-start = (f32[48,512]{1,0:T(8,128)S(1)}, f32[48,512]{1,0:T(8,128)S(1)}, u32[]{:S(2)}, u32[]{:S(2)}) collective-permute-start(f32[48,512]{1,0:T(8,128)S(1)} %get-tuple-element.8), channel_id=1, source_target_pairs={{0,1},{1,0},{2,3},{3,2},{4,5},{5,4},{6,7},{7,6},{8,9},{9,8},{10,11... | collective-permute-start | bytes 294920 | tf_op jit(solution)/shard_map/ppermute | solution.py:223
  6.7 2.8 %collective-permute-done = f32[48,512]{1,0:T(8,128)S(1)} collective-permute-done((f32[48,512]{1,0:T(8,128)S(1)}, f32[48,512]{1,0:T(8,128)S(1)}, u32[]{:S(2)}, u32[]{:S(2)}) %collective-permute-start) | collective-permute-done | bytes 98336 | tf_op jit(solution)/shard_map/ppermute | solution.py:223
  9.5 0.1 shard_map.38
  9.6 24.3 %all_to_all.5.x_ref = bf16[16,40,512]{2,1,0:T(8,128)(2,1)S(1)} all-to-all(bf16[16,40,512]{2,1,0:T(8,128)(2,1)S(1)} %shard_map.38), channel_id=1, replica_groups=mesh['tm'=16,'sec'=2] {'tm'}, dimensions={0} | all-to-all | bytes 1310720 | tf_op jit(solution)/shard_map/all_to_all | solution.py:236
  33.8 9.9 %shard_map.39 = f32[384,513]{1,0:T(8,128)} custom-call(bf16[16,40,512]{2,1,0:T(8,128)(2,1)S(1)} %all_to_all.5.x_ref), custom_call_target="tpu_custom_call" | custom-call | tf_op jit(solution)/shard_map/pallas_call | solution.py:203
  (2 shorter events, 0.0 us)
Async XLA Ops:
  0.0 1.1 %copy-start = (f32[384,512]{1,0:T(8,128)S(1)}, f32[384,512]{1,0:T(8,128)}, u32[]{:S(2)}) copy-start(f32[384,512]{1,0:T(8,128)} %rec_ref.1) | copy-start | bytes 2359300
  1.1 0.7 %copy-start.1 = (s32[16]{0:T(128)S(1)}, s32[16]{0:T(128)}, u32[]{:S(2)}) copy-start(s32[16]{0:T(128)} %index_ref.1) | copy-start | bytes 196
  1.8 0.7 %copy-start.2 = (f32[65]{0:T(128)S(1)}, f32[65]{0:T(128)}, u32[]{:S(2)}) copy-start(f32[65]{0:T(128)} %taps_ref.1) | copy-start | bytes 784
  3.7 5.8 %collective-permute-start = (f32[48,512]{1,0:T(8,128)S(1)}, f32[48,512]{1,0:T(8,128)S(1)}, u32[]{:S(2)}, u32[]{:S(2)}) collective-permute-start(f32[48,512]{1,0:T(8,128)S(1)} %get-tuple-element.8), channel_id=1, source_target_pairs={{0,1},{1,0},{2,3},{3,2},{4,5},{5,4},{6,7},{7,6},{8,9},{9,8},{10,11... | collective-permute-start | bytes 294920 | tf_op jit(solution)/shard_map/ppermute | solution.py:223

commit v2 on v1

--- a/solution.py
+++ b/solution.py
@@ -119,99 +119,99 @@
     )(filt, pilots, low, high)
 
 
-def corr_kernel(x_ref, o_ref, p_ref, z_ref, acc_ref, os_ref, *, kc, count):
+def corr_kernel(x_ref, o_ref, lo_ref, v_ref, z_ref, acc_ref, *, kc, count):
     wins, _, win = x_ref.shape
     T=wins*win
-    p_ref[:, :128]=jnp.zeros((16,128),p_ref.dtype)
-    p_ref[:, 128+T:]=jnp.zeros((16,p_ref.shape[1]-128-T),p_ref.dtype)
+    KT=T+256
+    nt=T//128
+    per=win//128
     esum=jnp.zeros((16,128),f32)
     usum=jnp.zeros((count,128),f32)
-    for w in range(wins):
-        pw=x_ref[w,0:16,:]
-        p_ref[:,128+w*win:128+(w+1)*win]=pw.astype(p_ref.dtype)
-        uw=x_ref[w,16:16+count,:].astype(f32)
-        pf=pw.astype(f32)
-        for q in range(win//128):
-            s=slice(q*128,(q+1)*128)
-            esum=esum+pf[:,s]*pf[:,s]; usum=usum+uw[:,s]*uw[:,s]
-    nz=z_ref.shape[0]//128
-    zero=jnp.zeros((count,128),f32)
-    def utile(k):
-        k=k-2
-        if k<0 or k>=T//128: return zero
-        w,q=divmod(k*128,win)
-        return x_ref[w,16:16+count,q:q+128].astype(f32)
-    lane=lax.broadcasted_iota(jnp.int32,(count,128),1)
-    padrows=jnp.zeros((32-count,128),f32)
-    rolled=None
-    for k in range(nz+1):
-        t=utile(k)
-        nxt=[t]+[pltpu.roll(t,128-32*r,1) for r in (1,2,3)]
-        if rolled is not None:
-            parts=[]
-            for r in range(4):
-                v=rolled[r] if r==0 else jnp.where(lane<128-32*r, rolled[r], nxt[r])
-                parts+= [v,padrows]
-            blk=jnp.concatenate(parts,axis=0)
-            z_ref[(k-1)*128:k*128,:]=blk.T.astype(bf16)
-        rolled=nxt
-    acc_ref[...]=jnp.zeros_like(acc_ref)
-    steps=-(-(T+G)//kc)
-    def body(i,_):
-        t0=pl.multiple_of(i*kc,kc)
-        X=p_ref[:,pl.ds(t0,kc+128)]
-        rows=[]
-        for j in range(G+1):
-            rows.append((pltpu.roll(X,j,1) if j else X)[:,128:].astype(bf16))
+    zlo=jnp.zeros((16,256),bf16)
+    lo_ref[:,:256]=zlo
+    lo_ref[:,256+T:]=zlo[:,:128]
+    v_ref[:,:128]=zlo[:,:128]
+    v_ref[:,256+T:]=zlo[:,:128]
+    lane8=lax.broadcasted_iota(jnp.int32,(8,128),1)
+    def him(a,b):
+        return jnp.concatenate([a,jnp.where(lane8<112,pltpu.roll(a,112,1),pltpu.roll(b,112,1))],axis=0).astype(bf16)
+    z8=jnp.zeros((8,128),f32)
+    prev=z8
+    for k in range(nt):
+        w,q=divmod(k,per); s=slice(q*128,q*128+128)
+        p=x_ref[w,0:16,s].astype(f32)
+        u=x_ref[w,16:16+count,s].astype(f32)
+        esum=esum+p*p; usum=usum+u*u
+        lo_ref[:,256+128*k:384+128*k]=x_ref[w,16:32,s]
+        v_ref[:,128+128*k:256+128*k]=him(prev,u[16:])
+        prev=u[16:]
+    v_ref[:,128+T:256+T]=him(prev,z8)
+    lane=lax.broadcasted_iota(jnp.int32,(16,128),1)
+    zp=jnp.zeros((16,128),bf16)
+    for q in range(4): z_ref[q,:,:512]=jnp.zeros((16,512),bf16)
+    def ptile(k):
+        if k>=nt: return zp
+        w,q=divmod(k,per)
+        return x_ref[w,0:16,q*128:q*128+128]
+    state=[[zp]*4,[zp]*4]
+    def zbuild(k):
+        t=ptile(k)
+        rolls=[t]+[pltpu.roll(t,32*q,1) for q in (1,2,3)]
+        S=[t]+[jnp.where(lane<32*q,state[0][q],rolls[q]) for q in (1,2,3)]
+        for q in range(4): z_ref[q,:,512+128*k:640+128*k]=S[q]
+        state[0]=rolls; state[1]=S
+    steps=-(-KT//kc)
+    def chunk(t0,first):
+        X=lo_ref[:,pl.ds(t0,kc+128)]
+        V=v_ref[:,pl.ds(t0,kc+128)]
+        w=kc+128
+        rows=[(pltpu.roll(X,w-j,1) if j else X)[:,:kc] for j in range(G+1)]
+        rows+=[(pltpu.roll(V,w-j,1) if j else V)[:,:kc] for j in range(G//2)]
+        rows.append(pltpu.roll(V,w-16,1)[:,:kc])
         plate=jnp.concatenate(rows,axis=0)
-        rhs=jnp.concatenate([z_ref[pl.ds(pl.multiple_of(t0+128*a,128),kc),:] for a in range(4)],axis=1)
-        d=jnp.dot(plate,rhs,preferred_element_type=f32)
-        for a in range(4): acc_ref[a]+=d[:,128*a:128*a+128]
-        return 0
-    lax.fori_loop(0,steps,body,0)
+        rhs=jnp.concatenate([z_ref[g%4,:,pl.ds(t0+512-128*(g//4),kc)] for g in range(16)],axis=0)
+        d=lax.dot_general(plate,rhs,(((1,),(1,)),((),())),preferred_element_type=f32)
+        for a in range(2):
+            if first: acc_ref[a]=d[:,128*a:128*a+128]
+            else: acc_ref[a]+=d[:,128*a:128*a+128]
+    for i in range(steps):
+        for k in range(i*kc//128,(i+1)*kc//128): zbuild(k)
+        chunk(i*kc,i==0)
     es=lax.rsqrt(jnp.sum(esum,axis=1,keepdims=True)/T+EPS)
     ue=lax.rsqrt(jnp.sum(usum,axis=1,keepdims=True)/T+EPS)/math.sqrt(T)
-    lane=lax.broadcasted_iota(jnp.int32,(count,128),1)
-    for quad in range(4):
-        scl=[jnp.broadcast_to(ue*jnp.broadcast_to(es[4*quad+m:4*quad+m+1],(count,1)),(count,128)) for m in range(4)]
-        for a in range(4):
-            blk=jnp.concatenate([acc_ref[a,pl.ds(4*quad+m,32,stride=16),:] for m in range(4)],axis=0)
-            Y=blk.T
-            for m in range(4):
-                o=None
-                for r in range(4):
-                    v=Y[32*r:32*r+count,:]
-                    sh=(32*(r-m))%128
-                    v=pltpu.roll(v,sh,1) if sh else v
-                    o=v if o is None else jnp.where(lane<32*r,o,v)
-                os_ref[a,pl.ds(4*quad+m,count,stride=16),:]=o*scl[m]
-    last=acc_ref[3,512:528,:]
-    last=pltpu.roll(last,32,1)
-    last=jnp.concatenate([last*es]+[jnp.zeros((112,128),f32)],axis=0).T[:count]*ue
-    for s in range(16):
-        v=pltpu.roll(last,(128-s)%128,1) if s else last
-        os_ref[4,pl.ds(s,count,stride=16),:]=v
-    for a in range(4): o_ref[:,128*a:128*a+128]=os_ref[a]
-    o_ref[:,512:513]=os_ref[4][:,0:1]
-
-def correlate(x):
-    wins, rows, win = x.shape
-    count = rows - 16
-    samples = wins * win
-    kc = 1664
-    steps = -(-(samples + G) // kc)
-    out = pl.pallas_call(
-        functools.partial(corr_kernel, kc=kc, count=count),
-        out_shape=jax.ShapeDtypeStruct((count * 16, NLAG), f32),
-        scratch_shapes=[
-            pltpu.VMEM((16, steps * kc + 128), bf16),
-            pltpu.VMEM((steps * kc + 384, 128), bf16),
-            pltpu.VMEM((4, (G + 1) * 16, 128), f32),
-            pltpu.VMEM((5, count * 16, 128), f32),
-        ],
-        compiler_params=pltpu.CompilerParams(vmem_limit_bytes=48 * 1024 * 1024),
+    esb=jnp.broadcast_to(es,(16,128))
+    hi0=16*(G+1)
+    def lags(h,c):
+        if c<16: return acc_ref[h,pl.ds(c,32,stride=16),:]
+        return jnp.concatenate([acc_ref[h,pl.ds(hi0+c-16,16,stride=16),:],acc_ref[h,pl.ds(hi0+c-8,16,stride=16),:]],axis=0)
+    for quad in range(count//4):
+        scl=[esb*jnp.broadcast_to(ue[4*quad+m:4*quad+m+1],(16,128)) for m in range(4)]
+        for h in range(2):
+            Y=jnp.concatenate([lags(h,4*quad+m) for m in range(4)],axis=0).T
+            for b in range(2):
+                for m in range(4):
+                    o=None
+                    for q in range(4):
+                        v=Y[64*b+16*q:64*b+16*q+16,:]
+                        sh=(32*(q-m))%128
+                        v=pltpu.roll(v,sh,1) if sh else v
+                        o=v if o is None else jnp.where(lane<32*q,o,v)
+                    o_ref[4*quad+m,:,(2*h+b)*128:(2*h+b)*128+128]=o*scl[m]
+    last=jnp.concatenate([acc_ref[1,512:528,:],acc_ref[1,hi0+264:hi0+272,:]],axis=0)
+    last=jnp.concatenate([last*ue,jnp.zeros((104,128),f32)],axis=0).T[112:128]*es
+    for c in range(count):
+        v=pltpu.roll(last,128-c,1) if c else last
+        o_ref[c,:,512:513]=v[:,0:1]
+def correlate(x,kc=2816):
+    wins,rows,win=x.shape
+    count=rows-16
+    T=wins*win
+    out=pl.pallas_call(functools.partial(corr_kernel,kc=kc,count=count),
+        out_shape=jax.ShapeDtypeStruct((count,16,NLAG),f32),
+        scratch_shapes=[pltpu.VMEM((16,T+384),bf16),pltpu.VMEM((16,T+384),bf16),pltpu.VMEM((4,16,T+768),bf16),pltpu.VMEM((2,16*(3*G//2+2),128),f32)],
+        compiler_params=pltpu.CompilerParams(vmem_limit_bytes=48*1024*1024),
     )(x)
-    return out.reshape(count, 16, NLAG)
+    return out
 
 
 def shards(record, fir_taps, source_index):

time: 43.9 us -> 40.9 us (0.932)
  Pallas kernels: 11.1 us -> 8.13 us
    pallas_call x1, Pallas kernels: 9.86 us -> 6.86 us  [correlate(): pl.pallas_call(functools.partial(corr_kernel, kc=kc, count=count), out_sh...]
where the time goes in v2:
time: 40.9 us; the launch traced here: 40.7 us
  blocking collectives  24.3 us (59%)
  Pallas kernels  8.13 us (20%)
  starting transfers between devices  3.03 us (7%)
  waiting for transfers between devices  2.79 us (7%)
  local copies, waits for them, and re-layouts  2.44 us (6%)
    all_to_all x1, blocking collectives, shards(): return correlate(lax.all_to_all(blocks, 'tm', 0, 0, tiled=True))  24.3 us
    pallas_call x1, Pallas kernels, correlate(): pl.pallas_call(functools.partial(corr_kernel, kc=kc, count=count), out_sh...  6.86 us
    ppermute x1, starting transfers between devices, shards(): other = lax.ppermute(exch, 'sec', [(0, 1), (1, 0)])  3.03 us
    ppermute x1, waiting for transfers between devices, shards(): other = lax.ppermute(exch, 'sec', [(0, 1), (1, 0)])  2.79 us
    unnamed x6, local copies, waits for them, and re-layouts  2.44 us
    pallas_call x1, Pallas kernels, filter_rows(): pl.pallas_call(functools.partial(filter_kernel, pair=pair), out_shape=(ja...  1.22 us
  transfers between devices with their start and end apart: 1, of which 1 were waited for; matrix products, arithmetic and copies ran while one was open for 0% of the time, Pallas kernels for 0%

profile of v2, /device:TPU:0, one launch (start us, length us, event | category | flops | bytes accessed | tf_op | source)
XLA Modules:
  0.0 40.7 jit_solution(18359585405512472452)
XLA Ops:
  0.0 0.0 copy-start
  0.0 1.1 %copy-done = f32[384,512]{1,0:T(8,128)S(1)} copy-done((f32[384,512]{1,0:T(8,128)S(1)}, f32[384,512]{1,0:T(8,128)}, u32[]{:S(2)}) %copy-start) | copy-done | bytes 786456
  1.1 0.0 copy-start.1
  1.1 0.7 %copy-done.1 = s32[16]{0:T(128)S(1)} copy-done((s32[16]{0:T(128)S(1)}, s32[16]{0:T(128)}, u32[]{:S(2)}) %copy-start.1) | copy-done | bytes 88
  1.8 0.0 copy-start.2
  1.8 0.7 %copy-done.2 = f32[65]{0:T(128)S(1)} copy-done((f32[65]{0:T(128)S(1)}, f32[65]{0:T(128)}, u32[]{:S(2)}) %copy-start.2) | copy-done | bytes 284
  2.4 1.2 %shard_map.37 = (f32[384,512]{1,0:T(8,128)S(1)}, f32[48,512]{1,0:T(8,128)S(1)}) custom-call(s32[16]{0:T(128)S(1)} %copy-done.1, f32[65]{0:T(128)S(1)} %copy-done.2, f32[384,512]{1,0:T(8,128)S(1)} %copy-done), custom_call_target="tpu_custom_call" | custom-call | tf_op jit(solution)/shard_map/pallas_call | solution.py:73
  3.7 3.0 %collective-permute-start = (f32[48,512]{1,0:T(8,128)S(1)}, f32[48,512]{1,0:T(8,128)S(1)}, u32[]{:S(2)}, u32[]{:S(2)}) collective-permute-start(f32[48,512]{1,0:T(8,128)S(1)} %get-tuple-element.8), channel_id=1, source_target_pairs={{0,1},{1,0},{2,3},{3,2},{4,5},{5,4},{6,7},{7,6},{8,9},{9,8},{10,11... | collective-permute-start | bytes 294920 | tf_op jit(solution)/shard_map/ppermute | solution.py:223
  6.7 2.8 %collective-permute-done = f32[48,512]{1,0:T(8,128)S(1)} collective-permute-done((f32[48,512]{1,0:T(8,128)S(1)}, f32[48,512]{1,0:T(8,128)S(1)}, u32[]{:S(2)}, u32[]{:S(2)}) %collective-permute-start) | collective-permute-done | bytes 98336 | tf_op jit(solution)/shard_map/ppermute | solution.py:223
  9.5 0.1 shard_map.38
  9.6 24.3 %all_to_all.5.x_ref = bf16[16,40,512]{2,1,0:T(8,128)(2,1)S(1)} all-to-all(bf16[16,40,512]{2,1,0:T(8,128)(2,1)S(1)} %shard_map.38), channel_id=1, replica_groups=mesh['tm'=16,'sec'=2] {'tm'}, dimensions={0} | all-to-all | bytes 1310720 | tf_op jit(solution)/shard_map/all_to_all | solution.py:236
  33.8 6.9 %shard_map.39 = f32[24,16,513]{2,1,0:T(8,128)} custom-call(bf16[16,40,512]{2,1,0:T(8,128)(2,1)S(1)} %all_to_all.5.x_ref), custom_call_target="tpu_custom_call" | custom-call | tf_op jit(solution)/shard_map/pallas_call | solution.py:209
  (2 shorter events, 0.0 us)
Async XLA Ops:
  0.0 1.1 %copy-start = (f32[384,512]{1,0:T(8,128)S(1)}, f32[384,512]{1,0:T(8,128)}, u32[]{:S(2)}) copy-start(f32[384,512]{1,0:T(8,128)} %rec_ref.1) | copy-start | bytes 2359300
  1.1 0.7 %copy-start.1 = (s32[16]{0:T(128)S(1)}, s32[16]{0:T(128)}, u32[]{:S(2)}) copy-start(s32[16]{0:T(128)} %index_ref.1) | copy-start | bytes 196
  1.8 0.7 %copy-start.2 = (f32[65]{0:T(128)S(1)}, f32[65]{0:T(128)}, u32[]{:S(2)}) copy-start(f32[65]{0:T(128)} %taps_ref.1) | copy-start | bytes 784
  3.7 5.8 %collective-permute-start = (f32[48,512]{1,0:T(8,128)S(1)}, f32[48,512]{1,0:T(8,128)S(1)}, u32[]{:S(2)}, u32[]{:S(2)}) collective-permute-start(f32[48,512]{1,0:T(8,128)S(1)} %get-tuple-element.8), channel_id=1, source_target_pairs={{0,1},{1,0},{2,3},{3,2},{4,5},{5,4},{6,7},{7,6},{8,9},{9,8},{10,11... | collective-permute-start | bytes 294920 | tf_op jit(solution)/shard_map/ppermute | solution.py:223

commit v3 on v2

--- a/solution.py
+++ b/solution.py
@@ -16,40 +16,64 @@
 EPS = 1e-6 * SCALE * SCALE
 G = 32
 HALO = 32
-SMEM = pltpu.SMEM
-VMEM = pltpu.VMEM
-
-
-def filter_kernel(index_ref, taps_ref, rec_ref, filt_ref, exch_ref, hi_ref, lo_ref, ext_ref, *, pair):
-    rows, width = rec_ref.shape
-    taps = taps_ref.shape[0]
-    sources = index_ref.shape[0]
+FETCHES = 3
+VMEM_ALL = 64 * 1024 * 1024
+
+
+def band_halves(taps_ref, shift):
     lane = lax.broadcasted_iota(jnp.int32, (8, 256), 1)
     base = jnp.zeros((8, 256), f32)
-    for m in range(taps):
+    for m in range(taps_ref.shape[0]):
         base = jnp.where(lane == m, taps_ref[m] * SCALE, base)
     tall = jnp.concatenate([base] * 16, axis=0)
-    band = pltpu.roll(tall, 0, 1, stride=1, stride_axis=0)
-    band_hi = band.astype(bf16)
-    band_lo = (band - band_hi.astype(f32)).astype(bf16)
-    both = jnp.concatenate([band_hi, band_lo], axis=0)
-    edge = jnp.zeros((64, width), bf16)
-    tiles = -(-(rows + 64) // 128)
-    spare = hi_ref.shape[0] - 64 - rows
-    for ref in (hi_ref, lo_ref):
-        ref[:64, :] = edge
-        ref[64 + rows :, :] = jnp.zeros((spare, width), bf16)
-    rec = rec_ref[...]
-    rec_hi = rec.astype(bf16)
-    hi_ref[64 : 64 + rows, :] = rec_hi
-    lo_ref[64 : 64 + rows, :] = (rec - rec_hi.astype(f32)).astype(bf16)
-    for i in range(tiles):
-        hi = hi_ref[128 * i : 128 * i + 256, :]
-        lo = lo_ref[128 * i : 128 * i + 256, :]
-        big = jnp.dot(both, hi, preferred_element_type=f32)
-        small = jnp.dot(band_hi, lo, preferred_element_type=f32)
-        ext_ref[128 * i : 128 * i + 128, :] = big[:128] + (big[128:] + small)
-    filt_ref[...] = ext_ref[HALO : HALO + rows, :]
+    band = pltpu.roll(tall, shift, 1, stride=1, stride_axis=0)
+    high = band.astype(bf16)
+    return high, (band - high.astype(f32)).astype(bf16)
+
+
+def clear_edges(refs, rows):
+    for ref in refs:
+        deep, width = ref.shape
+        ref[:64, :] = jnp.zeros((64, width), bf16)
+        ref[64 + rows :, :] = jnp.zeros((deep - 64 - rows, width), bf16)
+
+
+def split_rows(rec, hi_ref, lo_ref, at):
+    high = rec.astype(bf16)
+    hi_ref[at : at + rec.shape[0], :] = high
+    lo_ref[at : at + rec.shape[0], :] = (rec - high.astype(f32)).astype(bf16)
+
+
+def band_product(band, hi_ref, lo_ref, i):
+    hi = hi_ref[128 * i : 128 * i + 256, :]
+    lo = lo_ref[128 * i : 128 * i + 256, :]
+    big = jnp.dot(jnp.concatenate(band, axis=0), hi, preferred_element_type=f32)
+    small = jnp.dot(band[0], lo, preferred_element_type=f32)
+    return big[:128] + (big[128:] + small)
+
+
+def share_kernel(
+    index_hbm, taps_hbm, rec_hbm, exch_ref, index_ref, taps_ref, rec_ref, hi_ref, lo_ref, ext_ref, sems, *, pair
+):
+    rows, width = rec_ref.shape
+    sources = index_ref.shape[0]
+    step = rows // FETCHES
+    fetches = [pltpu.make_async_copy(taps_hbm, taps_ref, sems.at[FETCHES + 1])]
+    for i in range(FETCHES):
+        part = pl.ds(i * step, step)
+        fetches.append(pltpu.make_async_copy(rec_hbm.at[part, :], rec_ref.at[part, :], sems.at[i]))
+    fetches.append(pltpu.make_async_copy(index_hbm, index_ref, sems.at[FETCHES]))
+    for fetch in fetches:
+        fetch.start()
+    clear_edges((hi_ref, lo_ref), rows)
+    fetches[0].wait()
+    band = band_halves(taps_ref, 0)
+    for i in range(FETCHES):
+        fetches[1 + i].wait()
+        split_rows(rec_ref[i * step : (i + 1) * step, :], hi_ref, lo_ref, 64 + i * step)
+    fetches[1 + FETCHES].wait()
+    for i in range(ext_ref.shape[0] // 128):
+        ext_ref[128 * i : 128 * i + 128, :] = band_product(band, hi_ref, lo_ref, i)
     first = lax.axis_index("sec") * rows - HALO
     for s in range(sources):
         row = index_ref[s] - first
@@ -65,58 +89,86 @@
         exch_ref[sources + HALO :, :] = up
 
 
-def filter_rows(record, fir_taps, source_index, pair):
+def share(record, fir_taps, source_index, pair):
     rows, width = record.shape
     sources = source_index.shape[0]
     tiles = -(-(rows + 64) // 128)
-    deep = 128 * (tiles + 1)
     return pl.pallas_call(
-        functools.partial(filter_kernel, pair=pair),
-        out_shape=(
-            jax.ShapeDtypeStruct((rows, width), f32),
-            jax.ShapeDtypeStruct((sources + HALO * (1 if pair else 2), width), f32),
-        ),
-        in_specs=[
-            pl.BlockSpec(memory_space=SMEM),
-            pl.BlockSpec(memory_space=SMEM),
-            pl.BlockSpec(memory_space=VMEM),
+        functools.partial(share_kernel, pair=pair),
+        out_shape=jax.ShapeDtypeStruct((sources + HALO * (1 if pair else 2), width), f32),
+        in_specs=[pl.BlockSpec(memory_space=pltpu.HBM)] * 3,
+        scratch_shapes=[
+            pltpu.SMEM(source_index.shape, jnp.int32),
+            pltpu.SMEM(fir_taps.shape, f32),
+            pltpu.VMEM((rows, width), f32),
+            pltpu.VMEM((128 * (tiles + 1), width), bf16),
+            pltpu.VMEM((128 * (tiles + 1), width), bf16),
+            pltpu.VMEM((128 * tiles, width), f32),
+            pltpu.SemaphoreType.DMA((FETCHES + 2,)),
         ],
-        scratch_shapes=[
-            pltpu.VMEM((deep, width), bf16),
-            pltpu.VMEM((deep, width), bf16),
-            pltpu.VMEM((128 * tiles, width), f32),
-        ],
+        compiler_params=pltpu.CompilerParams(vmem_limit_bytes=VMEM_ALL),
+        cost_estimate=pl.CostEstimate(flops=2 * 3 * 128 * tiles * 256 * width, bytes_accessed=4 * rows * width, transcendentals=0),
+    )(source_index, fir_taps, record)
+
+
+def filter_kernel(taps_ref, rec_ref, filt_ref, hi_ref, lo_ref):
+    rows = rec_ref.shape[0]
+    clear_edges((hi_ref, lo_ref), rows)
+    band = band_halves(taps_ref, HALO)
+    split_rows(rec_ref[...], hi_ref, lo_ref, 64)
+    for i in range(rows // 128):
+        filt_ref[128 * i : 128 * i + 128, :] = band_product(band, hi_ref, lo_ref, i)
+
+
+def filter_rows(record, fir_taps):
+    rows, width = record.shape
+    return pl.pallas_call(
+        filter_kernel,
+        out_shape=jax.ShapeDtypeStruct((rows, width), f32),
+        in_specs=[pl.BlockSpec(memory_space=pltpu.SMEM), pl.BlockSpec(memory_space=pltpu.VMEM)],
+        scratch_shapes=[pltpu.VMEM((rows + 128, width), bf16), pltpu.VMEM((rows + 128, width), bf16)],
         compiler_params=pltpu.CompilerParams(vmem_limit_bytes=24 * 1024 * 1024),
-    )(source_index, fir_taps, record)
-
-
-def pack_kernel(filt_ref, pilots_ref, low_ref, high_ref, out_ref, *, count):
+        cost_estimate=pl.CostEstimate(flops=2 * 3 * rows * 256 * width, bytes_accessed=8 * rows * width, transcendentals=0),
+    )(fir_taps, record)
+
+
+def pack_kernel(filt_ref, *refs, count, sources, pair):
     rows = filt_ref.shape[0]
-    pilots = pilots_ref[...].astype(bf16)
-    sources = pilots.shape[0]
+    out_ref = refs[-1]
+    if pair:
+        here_ref, there_ref = refs[:2]
+        pilots = here_ref[:sources, :] + there_ref[:sources, :]
+        edge = there_ref[sources:, :]
+        second = lax.axis_index("sec") == 1
+        low = jnp.where(second, edge, 0.0)
+        high = jnp.where(second, 0.0, edge)
+    else:
+        pilots, low, high = (ref[...] for ref in refs[:3])
+    pilots = pilots.astype(bf16)
     for d in range(out_ref.shape[0]):
         out_ref[d, :sources, :] = pilots
         lo, hi = d * count, (d + 1) * count
         part = filt_ref[lo:hi, :]
         if lo < HALO:
             n = min(hi, HALO) - lo
-            add = low_ref[lo : lo + n, :]
+            add = low[lo : lo + n, :]
             part = jnp.concatenate([part[:n] + add, part[n:]], axis=0) if n < count else part + add
         if hi > rows - HALO:
-            n = hi - max(lo, rows - HALO)
-            add = high_ref[max(lo, rows - HALO) - (rows - HALO) : hi - (rows - HALO), :]
+            start = max(lo, rows - HALO)
+            add = high[start - (rows - HALO) : hi - (rows - HALO), :]
+            n = hi - start
             part = jnp.concatenate([part[: count - n], part[count - n :] + add], axis=0) if n < count else part + add
         out_ref[d, sources:, :] = part.astype(bf16)
 
 
-def pack(filt, pilots, low, high, devices):
+def pack(filt, others, devices, sources, pair):
     rows, width = filt.shape
     count = rows // devices
     return pl.pallas_call(
-        functools.partial(pack_kernel, count=count),
-        out_shape=jax.ShapeDtypeStruct((devices, pilots.shape[0] + count, width), bf16),
+        functools.partial(pack_kernel, count=count, sources=sources, pair=pair),
+        out_shape=jax.ShapeDtypeStruct((devices, sources + count, width), bf16),
         compiler_params=pltpu.CompilerParams(vmem_limit_bytes=24 * 1024 * 1024),
-    )(filt, pilots, low, high)
+    )(filt, *others)
 
 
 def corr_kernel(x_ref, o_ref, lo_ref, v_ref, z_ref, acc_ref, *, kc, count):
@@ -218,21 +270,18 @@
     sections = lax.axis_size("sec")
     pair = sections == 2
     sources = source_index.shape[0]
-    filt, exch = filter_rows(record, fir_taps, source_index, pair)
+    exch = share(record, fir_taps, source_index, pair)
+    filt = filter_rows(record, fir_taps)
     if pair:
-        other = lax.ppermute(exch, "sec", [(0, 1), (1, 0)])
-        pilots = exch[:sources] + other[:sources]
-        here = lax.axis_index("sec")
-        edge = other[sources:]
-        low = jnp.where(here == 1, edge, 0.0)
-        high = jnp.where(here == 0, edge, 0.0)
+        others = (exch, lax.ppermute(exch, "sec", [(0, 1), (1, 0)]))
     else:
         pilots = lax.psum(exch[:sources], "sec")
         up = [(i, i + 1) for i in range(sections - 1)]
         down = [(i + 1, i) for i in range(sections - 1)]
         high = lax.ppermute(exch[sources : sources + HALO], "sec", down)
         low = lax.ppermute(exch[sources + HALO :], "sec", up)
-    blocks = pack(filt, pilots, low, high, lax.axis_size("tm"))
+        others = (pilots, low, high)
+    blocks = pack(filt, others, lax.axis_size("tm"), sources, pair)
     return correlate(lax.all_to_all(blocks, "tm", 0, 0, tiled=True))
 
 

time: 40.9 us -> 39.9 us (0.976)
  waiting for transfers between devices: 2.79 us -> 0.12 us
  Pallas kernels: 8.13 us -> 10.4 us
  local copies, waits for them, and re-layouts: 2.44 us -> 1.79 us
    ppermute x1, waiting for transfers between devices: 2.79 us -> 0.12 us  [shards(): others = (exch, lax.ppermute(exch, 'sec', [(0, 1), (1, 0)]))]
    pallas_call x2 -> x3, Pallas kernels: 1.27 us -> 3.56 us  [the longest x1 2.42 us: share(): pl.pallas_call(functools.partial(share_kernel, pair=pair), out_shape=jax....]
    unnamed x6, local copies, waits for them, and re-layouts: 2.44 us -> 1.79 us
  transfers between devices with their start and end apart: 1 -> 1, of which waited for: 1 -> 1; matrix products, arithmetic and copies ran while one was open for 0% -> 0% of each run, Pallas kernels for 0% -> 3%
where the time goes in v3:
time: 39.9 us; the launch traced here: 39.6 us
  blocking collectives  24.2 us (61%)
  Pallas kernels  10.4 us (26%)
  starting transfers between devices  3.03 us (8%)
  local copies, waits for them, and re-layouts  1.79 us (4%)
    all_to_all x1, blocking collectives, shards(): return correlate(lax.all_to_all(blocks, 'tm', 0, 0, tiled=True))  24.2 us
    pallas_call x1, Pallas kernels, correlate(): pl.pallas_call(functools.partial(corr_kernel, kc=kc, count=count), out_sh...  6.86 us
    ppermute x1, starting transfers between devices, shards(): others = (exch, lax.ppermute(exch, 'sec', [(0, 1), (1, 0)]))  3.03 us
    pallas_call x1, Pallas kernels, share(): pl.pallas_call(functools.partial(share_kernel, pair=pair), out_shape=jax....  2.42 us
    unnamed x6, local copies, waits for them, and re-layouts  1.79 us
    pallas_call x1, Pallas kernels, filter_rows(): pl.pallas_call(filter_kernel, out_shape=jax.ShapeDtypeStruct((rows, width...  1.09 us
  transfers between devices with their start and end apart: 1, of which 1 were waited for; matrix products, arithmetic and copies ran while one was open for 0% of the time, Pallas kernels for 3%

profile of v3, /device:TPU:0, one launch (start us, length us, event | category | flops | bytes accessed | tf_op | source)
XLA Modules:
  0.0 39.6 jit_solution(12584558564204876735)
XLA Ops:
  0.0 2.4 %shard_map.38.refs_0_ = f32[48,512]{1,0:T(8,128)} custom-call(s32[16]{0:T(128)} %index_hbm.1, f32[65]{0:T(128)} %taps_hbm.1, f32[384,512]{1,0:T(8,128)} %rec_hbm.1), custom_call_target="tpu_custom_call" | custom-call | flops 402653184 | bytes 786432 | tf_op jit(solution)/shard_map/pallas_call | solution.py:96
  2.4 3.0 %collective-permute-start = (f32[48,512]{1,0:T(8,128)}, f32[48,512]{1,0:T(8,128)S(1)}, u32[]{:S(2)}, u32[]{:S(2)}) collective-permute-start(f32[48,512]{1,0:T(8,128)} %shard_map.38.refs_0_), channel_id=1, source_target_pairs={{0,1},{1,0},{2,3},{3,2},{4,5},{5,4},{6,7},{7,6},{8,9},{9,8},{10,11... | collective-permute-start | bytes 294920 | tf_op jit(solution)/shard_map/ppermute | solution.py:276
  5.5 0.0 copy-start
  5.5 1.1 %copy-done = f32[384,512]{1,0:T(8,128)S(1)} copy-done((f32[384,512]{1,0:T(8,128)S(1)}, f32[384,512]{1,0:T(8,128)}, u32[]{:S(2)}) %copy-start) | copy-done | bytes 786456
  6.6 0.0 copy-start.2
  6.6 0.7 %copy-done.2 = f32[65]{0:T(128)S(1)} copy-done((f32[65]{0:T(128)S(1)}, f32[65]{0:T(128)}, u32[]{:S(2)}) %copy-start.2) | copy-done | bytes 284
  7.3 0.0 copy-start.1
  7.3 1.1 %shard_map.37.filt_ref = f32[384,512]{1,0:T(8,128)S(1)} custom-call(f32[65]{0:T(128)S(1)} %copy-done.2, f32[384,512]{1,0:T(8,128)S(1)} %copy-done), custom_call_target="tpu_custom_call" | custom-call | flops 301989888 | bytes 1572864 | tf_op jit(solution)/shard_map/pallas_call | solution.py:125
  8.3 0.1 collective-permute-done.refs_1_
  8.5 0.0 copy-done.1
  8.5 0.1 shard_map.39
  8.5 24.2 %all_to_all.5.x_ref = bf16[16,40,512]{2,1,0:T(8,128)(2,1)S(1)} all-to-all(bf16[16,40,512]{2,1,0:T(8,128)(2,1)S(1)} %shard_map.39), channel_id=1, replica_groups=mesh['tm'=16,'sec'=2] {'tm'}, dimensions={0} | all-to-all | bytes 1310720 | tf_op jit(solution)/shard_map/all_to_all | solution.py:285
  32.8 6.9 %shard_map.40 = f32[24,16,513]{2,1,0:T(8,128)} custom-call(bf16[16,40,512]{2,1,0:T(8,128)(2,1)S(1)} %all_to_all.5.x_ref), custom_call_target="tpu_custom_call" | custom-call | tf_op jit(solution)/shard_map/pallas_call | solution.py:261
Async XLA Ops:
  2.4 6.0 %collective-permute-start = (f32[48,512]{1,0:T(8,128)}, f32[48,512]{1,0:T(8,128)S(1)}, u32[]{:S(2)}, u32[]{:S(2)}) collective-permute-start(f32[48,512]{1,0:T(8,128)} %shard_map.38.refs_0_), channel_id=1, source_target_pairs={{0,1},{1,0},{2,3},{3,2},{4,5},{5,4},{6,7},{7,6},{8,9},{9,8},{10,11... | collective-permute-start | bytes 294920 | tf_op jit(solution)/shard_map/ppermute | solution.py:276
  5.5 1.1 %copy-start = (f32[384,512]{1,0:T(8,128)S(1)}, f32[384,512]{1,0:T(8,128)}, u32[]{:S(2)}) copy-start(f32[384,512]{1,0:T(8,128)} %rec_hbm.1) | copy-start | bytes 2359300
  6.6 0.7 %copy-start.2 = (f32[65]{0:T(128)S(1)}, f32[65]{0:T(128)}, u32[]{:S(2)}) copy-start(f32[65]{0:T(128)} %taps_hbm.1) | copy-start | bytes 784
  7.3 1.2 %copy-start.1 = (f32[48,512]{1,0:T(8,128)S(1)}, f32[48,512]{1,0:T(8,128)}, u32[]{:S(2)}) copy-start(f32[48,512]{1,0:T(8,128)} %shard_map.38.refs_0_) | copy-start | bytes 294916

commit v4 on v3

--- a/solution.py
+++ b/solution.py
@@ -16,6 +16,7 @@
 EPS = 1e-6 * SCALE * SCALE
 G = 32
 HALO = 32
+HALF = 8
 FETCHES = 3
 VMEM_ALL = 64 * 1024 * 1024
 
@@ -144,9 +145,8 @@
         high = jnp.where(second, 0.0, edge)
     else:
         pilots, low, high = (ref[...] for ref in refs[:3])
-    pilots = pilots.astype(bf16)
     for d in range(out_ref.shape[0]):
-        out_ref[d, :sources, :] = pilots
+        own = pilots[HALF * (d % 2) : HALF * (d % 2) + HALF]
         lo, hi = d * count, (d + 1) * count
         part = filt_ref[lo:hi, :]
         if lo < HALO:
@@ -158,7 +158,7 @@
             add = high[start - (rows - HALO) : hi - (rows - HALO), :]
             n = hi - start
             part = jnp.concatenate([part[: count - n], part[count - n :] + add], axis=0) if n < count else part + add
-        out_ref[d, sources:, :] = part.astype(bf16)
+        out_ref[d] = jnp.concatenate([own, part], axis=0).astype(bf16)
 
 
 def pack(filt, others, devices, sources, pair):
@@ -166,12 +166,12 @@
     count = rows // devices
     return pl.pallas_call(
         functools.partial(pack_kernel, count=count, sources=sources, pair=pair),
-        out_shape=jax.ShapeDtypeStruct((devices, sources + count, width), bf16),
+        out_shape=jax.ShapeDtypeStruct((devices, HALF + count, width), bf16),
         compiler_params=pltpu.CompilerParams(vmem_limit_bytes=24 * 1024 * 1024),
     )(filt, *others)
 
 
-def corr_kernel(x_ref, o_ref, lo_ref, v_ref, z_ref, acc_ref, *, kc, count):
+def corr_kernel(x_ref, other_ref, o_ref, p_ref, lo_ref, v_ref, z_ref, acc_ref, *, kc, count):
     wins, _, win = x_ref.shape
     T=wins*win
     KT=T+256
@@ -191,10 +191,12 @@
     prev=z8
     for k in range(nt):
         w,q=divmod(k,per); s=slice(q*128,q*128+128)
-        p=x_ref[w,0:16,s].astype(f32)
-        u=x_ref[w,16:16+count,s].astype(f32)
+        block=x_ref[w,:,s].astype(f32)
+        p=jnp.concatenate([block[:HALF],other_ref[w,:,s].astype(f32)],axis=0)
+        u=block[HALF:]
         esum=esum+p*p; usum=usum+u*u
-        lo_ref[:,256+128*k:384+128*k]=x_ref[w,16:32,s]
+        p_ref[:,128*k:128*k+128]=p.astype(bf16)
+        lo_ref[:,256+128*k:384+128*k]=u[:16].astype(bf16)
         v_ref[:,128+128*k:256+128*k]=him(prev,u[16:])
         prev=u[16:]
     v_ref[:,128+T:256+T]=him(prev,z8)
@@ -203,8 +205,7 @@
     for q in range(4): z_ref[q,:,:512]=jnp.zeros((16,512),bf16)
     def ptile(k):
         if k>=nt: return zp
-        w,q=divmod(k,per)
-        return x_ref[w,0:16,q*128:q*128+128]
+        return p_ref[:,128*k:128*k+128]
     state=[[zp]*4,[zp]*4]
     def zbuild(k):
         t=ptile(k)
@@ -233,6 +234,11 @@
     ue=lax.rsqrt(jnp.sum(usum,axis=1,keepdims=True)/T+EPS)/math.sqrt(T)
     esb=jnp.broadcast_to(es,(16,128))
     hi0=16*(G+1)
+    mine=pl.multiple_of(lax.axis_index("tm")%2*HALF,HALF)
+    theirs=pl.multiple_of(HALF-mine,HALF)
+    def put(c,at,v):
+        o_ref[c,pl.ds(mine,HALF),at:at+v.shape[1]]=v[:HALF]
+        o_ref[c,pl.ds(theirs,HALF),at:at+v.shape[1]]=v[HALF:]
     def lags(h,c):
         if c<16: return acc_ref[h,pl.ds(c,32,stride=16),:]
         return jnp.concatenate([acc_ref[h,pl.ds(hi0+c-16,16,stride=16),:],acc_ref[h,pl.ds(hi0+c-8,16,stride=16),:]],axis=0)
@@ -248,21 +254,21 @@
                         sh=(32*(q-m))%128
                         v=pltpu.roll(v,sh,1) if sh else v
                         o=v if o is None else jnp.where(lane<32*q,o,v)
-                    o_ref[4*quad+m,:,(2*h+b)*128:(2*h+b)*128+128]=o*scl[m]
+                    put(4*quad+m,(2*h+b)*128,o*scl[m])
     last=jnp.concatenate([acc_ref[1,512:528,:],acc_ref[1,hi0+264:hi0+272,:]],axis=0)
     last=jnp.concatenate([last*ue,jnp.zeros((104,128),f32)],axis=0).T[112:128]*es
     for c in range(count):
         v=pltpu.roll(last,128-c,1) if c else last
-        o_ref[c,:,512:513]=v[:,0:1]
-def correlate(x,kc=2816):
+        put(c,512,v[:,0:1])
+def correlate(x,other,kc=2816):
     wins,rows,win=x.shape
-    count=rows-16
+    count=rows-HALF
     T=wins*win
     out=pl.pallas_call(functools.partial(corr_kernel,kc=kc,count=count),
         out_shape=jax.ShapeDtypeStruct((count,16,NLAG),f32),
-        scratch_shapes=[pltpu.VMEM((16,T+384),bf16),pltpu.VMEM((16,T+384),bf16),pltpu.VMEM((4,16,T+768),bf16),pltpu.VMEM((2,16*(3*G//2+2),128),f32)],
+        scratch_shapes=[pltpu.VMEM((16,T),bf16),pltpu.VMEM((16,T+384),bf16),pltpu.VMEM((16,T+384),bf16),pltpu.VMEM((4,16,T+768),bf16),pltpu.VMEM((2,16*(3*G//2+2),128),f32)],
         compiler_params=pltpu.CompilerParams(vmem_limit_bytes=48*1024*1024),
-    )(x)
+    )(x,other)
     return out
 
 
@@ -282,7 +288,10 @@
         low = lax.ppermute(exch[sources + HALO :], "sec", up)
         others = (pilots, low, high)
     blocks = pack(filt, others, lax.axis_size("tm"), sources, pair)
-    return correlate(lax.all_to_all(blocks, "tm", 0, 0, tiled=True))
+    blocks = lax.all_to_all(blocks, "tm", 0, 0, tiled=True)
+    swap = [(i, i ^ 1) for i in range(lax.axis_size("tm"))]
+    other = lax.ppermute(blocks[:, :HALF], "tm", swap)
+    return correlate(blocks, other)
 
 
 def solution(mesh):

time: 39.9 us -> 37.6 us (0.942)
  blocking collectives: 24.2 us -> 20.5 us
  waiting for transfers between devices: 0.12 us -> 1.45 us
    all_to_all x1, blocking collectives: 24.2 us -> 20.5 us  [shards(): blocks = lax.all_to_all(blocks, 'tm', 0, 0, tiled=True)]
    ppermute x0 -> x1, waiting for transfers between devices: none -> 1.33 us  [shards(): other = lax.ppermute(blocks[:, :HALF], 'tm', swap)]
  transfers between devices with their start and end apart: 1 -> 2, of which waited for: 1 -> 2; matrix products, arithmetic and copies ran while one was open for 0% -> 0% of each run, Pallas kernels for 3% -> 3%
where the time goes in v4:
time: 37.6 us; the launch traced here: 37.3 us
  blocking collectives  20.5 us (55%)
  Pallas kernels  10.5 us (28%)
  starting transfers between devices  3.11 us (8%)
  local copies, waits for them, and re-layouts  1.8 us (5%)
  waiting for transfers between devices  1.45 us (4%)
    all_to_all x1, blocking collectives, shards(): blocks = lax.all_to_all(blocks, 'tm', 0, 0, tiled=True)  20.5 us
    pallas_call x1, Pallas kernels, correlate(): pl.pallas_call(functools.partial(corr_kernel, kc=kc, count=count), out_sh...  6.91 us
    ppermute x1, starting transfers between devices, shards(): others = (exch, lax.ppermute(exch, 'sec', [(0, 1), (1, 0)]))  3.03 us
    pallas_call x1, Pallas kernels, share(): pl.pallas_call(functools.partial(share_kernel, pair=pair), out_shape=jax....  2.42 us
    unnamed x6, local copies, waits for them, and re-layouts  1.79 us
    ppermute x1, waiting for transfers between devices, shards(): other = lax.ppermute(blocks[:, :HALF], 'tm', swap)  1.33 us
    pallas_call x1, Pallas kernels, filter_rows(): pl.pallas_call(filter_kernel, out_shape=jax.ShapeDtypeStruct((rows, width...  1.09 us
  transfers between devices with their start and end apart: 2, of which 2 were waited for; matrix products, arithmetic and copies ran while one was open for 0% of the time, Pallas kernels for 3%

profile of v4, /device:TPU:0, one launch (start us, length us, event | category | flops | bytes accessed | tf_op | source)
XLA Modules:
  0.0 37.3 jit_solution(2559587887063062781)
XLA Ops:
  0.0 2.4 %shard_map.38.refs_0_ = f32[48,512]{1,0:T(8,128)} custom-call(s32[16]{0:T(128)} %index_hbm.1, f32[65]{0:T(128)} %taps_hbm.1, f32[384,512]{1,0:T(8,128)} %rec_hbm.1), custom_call_target="tpu_custom_call" | custom-call | flops 402653184 | bytes 786432 | tf_op jit(solution)/shard_map/pallas_call | solution.py:97
  2.4 3.0 %collective-permute-start = (f32[48,512]{1,0:T(8,128)}, f32[48,512]{1,0:T(8,128)S(1)}, u32[]{:S(2)}, u32[]{:S(2)}) collective-permute-start(f32[48,512]{1,0:T(8,128)} %shard_map.38.refs_0_), channel_id=1, source_target_pairs={{0,1},{1,0},{2,3},{3,2},{4,5},{5,4},{6,7},{7,6},{8,9},{9,8},{10,11... | collective-permute-start | bytes 294920 | tf_op jit(solution)/shard_map/ppermute | solution.py:282
  5.5 0.0 copy-start
  5.5 1.1 %copy-done = f32[384,512]{1,0:T(8,128)S(1)} copy-done((f32[384,512]{1,0:T(8,128)S(1)}, f32[384,512]{1,0:T(8,128)}, u32[]{:S(2)}) %copy-start) | copy-done | bytes 786456
  6.6 0.0 copy-start.2
  6.6 0.7 %copy-done.2 = f32[65]{0:T(128)S(1)} copy-done((f32[65]{0:T(128)S(1)}, f32[65]{0:T(128)}, u32[]{:S(2)}) %copy-start.2) | copy-done | bytes 284
  7.3 0.0 copy-start.1
  7.3 1.1 %shard_map.37.filt_ref = f32[384,512]{1,0:T(8,128)S(1)} custom-call(f32[65]{0:T(128)S(1)} %copy-done.2, f32[384,512]{1,0:T(8,128)S(1)} %copy-done), custom_call_target="tpu_custom_call" | custom-call | flops 301989888 | bytes 1572864 | tf_op jit(solution)/shard_map/pallas_call | solution.py:126
  8.3 0.1 collective-permute-done.refs_1_
  8.5 0.0 copy-done.1
  8.5 0.1 shard_map.39
  8.5 20.5 %all_to_all.5.x_ref = bf16[16,32,512]{2,1,0:T(8,128)(2,1)S(1)} all-to-all(bf16[16,32,512]{2,1,0:T(8,128)(2,1)S(1)} %shard_map.39), channel_id=1, replica_groups=mesh['tm'=16,'sec'=2] {'tm'}, dimensions={0} | all-to-all | bytes 1048576 | tf_op jit(solution)/shard_map/all_to_all | solution.py:291
  29.0 0.1 collective-permute-start.1
  29.1 1.3 %collective-permute-done.1.other_ref = bf16[16,8,512]{2,1,0:T(8,128)(2,1)S(1)} collective-permute-done((bf16[16,8,512]{2,1,0:T(8,128)(2,1)S(1)}, bf16[16,8,512]{2,1,0:T(8,128)(2,1)S(1)}, u32[]{:S(2)}, u32[]{:S(2)}) %collective-permute-start.1) | collective-permute-done | bytes 131104 | tf_op jit(solution)/shard_map/ppermute | solution.py:293
  30.4 6.9 %shard_map.40 = f32[24,16,513]{2,1,0:T(8,128)} custom-call(bf16[16,32,512]{2,1,0:T(8,128)(2,1)S(1)} %all_to_all.5.x_ref, bf16[16,8,512]{2,1,0:T(8,128)(2,1)S(1)} %collective-permute-done.1.other_ref), custom_call_target="tpu_custom_call" | custom-call | tf_op jit(solution)/shard_map/pallas_call | solution.py:267
  (1 shorter events, 0.0 us)
Async XLA Ops:
  2.4 6.0 %collective-permute-start = (f32[48,512]{1,0:T(8,128)}, f32[48,512]{1,0:T(8,128)S(1)}, u32[]{:S(2)}, u32[]{:S(2)}) collective-permute-start(f32[48,512]{1,0:T(8,128)} %shard_map.38.refs_0_), channel_id=1, source_target_pairs={{0,1},{1,0},{2,3},{3,2},{4,5},{5,4},{6,7},{7,6},{8,9},{9,8},{10,11... | collective-permute-start | bytes 294920 | tf_op jit(solution)/shard_map/ppermute | solution.py:282
  5.5 1.1 %copy-start = (f32[384,512]{1,0:T(8,128)S(1)}, f32[384,512]{1,0:T(8,128)}, u32[]{:S(2)}) copy-start(f32[384,512]{1,0:T(8,128)} %rec_hbm.1) | copy-start | bytes 2359300
  6.6 0.7 %copy-start.2 = (f32[65]{0:T(128)S(1)}, f32[65]{0:T(128)}, u32[]{:S(2)}) copy-start(f32[65]{0:T(128)} %taps_hbm.1) | copy-start | bytes 784
  7.3 1.2 %copy-start.1 = (f32[48,512]{1,0:T(8,128)S(1)}, f32[48,512]{1,0:T(8,128)}, u32[]{:S(2)}) copy-start(f32[48,512]{1,0:T(8,128)} %shard_map.38.refs_0_) | copy-start | bytes 294916
  29.0 1.4 %collective-permute-start.1 = (bf16[16,8,512]{2,1,0:T(8,128)(2,1)S(1)}, bf16[16,8,512]{2,1,0:T(8,128)(2,1)S(1)}, u32[]{:S(2)}, u32[]{:S(2)}) collective-permute-start(bf16[16,8,512]{2,1,0:T(8,128)(2,1)S(1)} %slice.4), channel_id=1, source_target_pairs={{0,2},{2,0},{4,6},{6,4},{8,10},{10,8},{12,14},{14,12},{16,18},{18,... | collective-permute-start | bytes 393224 | tf_op jit(solution)/shard_map/ppermute | solution.py:293

commit v5 on v4

--- a/solution.py
+++ b/solution.py
@@ -17,8 +17,8 @@
 G = 32
 HALO = 32
 HALF = 8
+SENT = 4
 FETCHES = 3
-VMEM_ALL = 64 * 1024 * 1024
 
 
 def band_halves(taps_ref, shift):
@@ -107,7 +107,7 @@
             pltpu.VMEM((128 * tiles, width), f32),
             pltpu.SemaphoreType.DMA((FETCHES + 2,)),
         ],
-        compiler_params=pltpu.CompilerParams(vmem_limit_bytes=VMEM_ALL),
+        compiler_params=pltpu.CompilerParams(vmem_limit_bytes=24*1024*1024),
         cost_estimate=pl.CostEstimate(flops=2 * 3 * 128 * tiles * 256 * width, bytes_accessed=4 * rows * width, transcendentals=0),
     )(source_index, fir_taps, record)
 
@@ -171,7 +171,7 @@
     )(filt, *others)
 
 
-def corr_kernel(x_ref, other_ref, o_ref, p_ref, lo_ref, v_ref, z_ref, acc_ref, *, kc, count):
+def corr_kernel(x_ref, other_ref, out_hbm, o_ref, sems, p_ref, lo_ref, v_ref, z_ref, acc_ref, *, kc, count):
     wins, _, win = x_ref.shape
     T=wins*win
     KT=T+256
@@ -222,7 +222,7 @@
         rows+=[(pltpu.roll(V,w-j,1) if j else V)[:,:kc] for j in range(G//2)]
         rows.append(pltpu.roll(V,w-16,1)[:,:kc])
         plate=jnp.concatenate(rows,axis=0)
-        rhs=jnp.concatenate([z_ref[g%4,:,pl.ds(t0+512-128*(g//4),kc)] for g in range(16)],axis=0)
+        rhs=jnp.concatenate([z_ref[q,:,pl.ds(t0+512-128*a,kc)] for q in range(4) for a in range(4)],axis=0)
         d=lax.dot_general(plate,rhs,(((1,),(1,)),((),())),preferred_element_type=f32)
         for a in range(2):
             if first: acc_ref[a]=d[:,128*a:128*a+128]
@@ -242,31 +242,40 @@
     def lags(h,c):
         if c<16: return acc_ref[h,pl.ds(c,32,stride=16),:]
         return jnp.concatenate([acc_ref[h,pl.ds(hi0+c-16,16,stride=16),:],acc_ref[h,pl.ds(hi0+c-8,16,stride=16),:]],axis=0)
-    for quad in range(count//4):
-        scl=[esb*jnp.broadcast_to(ue[4*quad+m:4*quad+m+1],(16,128)) for m in range(4)]
-        for h in range(2):
-            Y=jnp.concatenate([lags(h,4*quad+m) for m in range(4)],axis=0).T
-            for b in range(2):
-                for m in range(4):
-                    o=None
-                    for q in range(4):
-                        v=Y[64*b+16*q:64*b+16*q+16,:]
-                        sh=(32*(q-m))%128
-                        v=pltpu.roll(v,sh,1) if sh else v
-                        o=v if o is None else jnp.where(lane<32*q,o,v)
-                    put(4*quad+m,(2*h+b)*128,o*scl[m])
     last=jnp.concatenate([acc_ref[1,512:528,:],acc_ref[1,hi0+264:hi0+272,:]],axis=0)
     last=jnp.concatenate([last*ue,jnp.zeros((104,128),f32)],axis=0).T[112:128]*es
     for c in range(count):
         v=pltpu.roll(last,128-c,1) if c else last
         put(c,512,v[:,0:1])
+    copies=[]
+    wide=lax.broadcasted_iota(jnp.int32,(32,128),1)<64
+    for c in range(0,count,2):
+        parts=[]
+        for h in range(2):
+            even,odd=lags(h,c),lags(h,c+1)
+            parts.append(jnp.where(wide,even,pltpu.roll(odd,64,1)))
+            parts.append(jnp.where(wide,pltpu.roll(even,64,1),odd))
+        turned=jnp.concatenate(parts,axis=0).T
+        for m in range(2):
+            scl=esb*jnp.broadcast_to(ue[c+m:c+m+1],(16,128))
+            for a in range(4):
+                put(c+m,128*a,turned[64*m+16*a:64*m+16*a+16,:]*scl)
+        if (c+2)%SENT==0:
+            group=pl.ds(c+2-SENT,SENT)
+            copies.append(pltpu.make_async_copy(o_ref.at[group],out_hbm.at[group],sems.at[c//SENT]))
+            copies[-1].start()
+    for copy in copies:
+        copy.wait()
+
+
 def correlate(x,other,kc=2816):
     wins,rows,win=x.shape
     count=rows-HALF
     T=wins*win
     out=pl.pallas_call(functools.partial(corr_kernel,kc=kc,count=count),
         out_shape=jax.ShapeDtypeStruct((count,16,NLAG),f32),
-        scratch_shapes=[pltpu.VMEM((16,T),bf16),pltpu.VMEM((16,T+384),bf16),pltpu.VMEM((16,T+384),bf16),pltpu.VMEM((4,16,T+768),bf16),pltpu.VMEM((2,16*(3*G//2+2),128),f32)],
+        out_specs=pl.BlockSpec(memory_space=pltpu.HBM),
+        scratch_shapes=[pltpu.VMEM((count,16,NLAG),f32),pltpu.SemaphoreType.DMA((count//SENT,)),pltpu.VMEM((16,T),bf16),pltpu.VMEM((16,T+384),bf16),pltpu.VMEM((16,T+384),bf16),pltpu.VMEM((4,16,T+768),bf16),pltpu.VMEM((2,16*(3*G//2+2),128),f32)],
         compiler_params=pltpu.CompilerParams(vmem_limit_bytes=48*1024*1024),
     )(x,other)
     return out
@@ -276,7 +285,8 @@
     sections = lax.axis_size("sec")
     pair = sections == 2
     sources = source_index.shape[0]
-    exch = share(record, fir_taps, source_index, pair)
+    hbm = [pltpu.with_memory_space_constraint(x, pltpu.HBM) for x in (record, fir_taps, source_index)]
+    exch = share(*hbm, pair)
     filt = filter_rows(record, fir_taps)
     if pair:
         others = (exch, lax.ppermute(exch, "sec", [(0, 1), (1, 0)]))

time: 37.6 us -> 35.9 us (0.955)
  local copies, waits for them, and re-layouts: 1.8 us -> 0.02 us
  waiting for transfers between devices: 1.45 us -> 3.02 us
  Pallas kernels: 10.5 us -> 9.04 us
    unnamed x6 -> x4, local copies, waits for them, and re-layouts: 1.79 us -> 0.01 us
    ppermute x1, waiting for transfers between devices: 0.12 us -> 1.69 us  [shards(): others = (exch, lax.ppermute(exch, 'sec', [(0, 1), (1, 0)]))]
    pallas_call x1, Pallas kernels: 6.91 us -> 6.04 us  [correlate(): pl.pallas_call(functools.partial(corr_kernel, kc=kc, count=count), out_sh...]
    pallas_call x1, Pallas kernels: 2.42 us -> 1.86 us  [share(): pl.pallas_call(functools.partial(share_kernel, pair=pair), out_shape=jax....]
where the time goes in v5:
time: 35.9 us; the launch traced here: 35.7 us
  blocking collectives  20.5 us (57%)
  Pallas kernels  9.04 us (25%)
  starting transfers between devices  3.11 us (9%)
  waiting for transfers between devices  3.02 us (8%)
    all_to_all x1, blocking collectives, shards(): blocks = lax.all_to_all(blocks, 'tm', 0, 0, tiled=True)  20.5 us
    pallas_call x1, Pallas kernels, correlate(): pl.pallas_call(functools.partial(corr_kernel, kc=kc, count=count), out_sh...  6.04 us
    ppermute x1, starting transfers between devices, shards(): others = (exch, lax.ppermute(exch, 'sec', [(0, 1), (1, 0)]))  3.03 us
    pallas_call x1, Pallas kernels, share(): pl.pallas_call(functools.partial(share_kernel, pair=pair), out_shape=jax....  1.86 us
    ppermute x1, waiting for transfers between devices, shards(): others = (exch, lax.ppermute(exch, 'sec', [(0, 1), (1, 0)]))  1.69 us
    ppermute x1, waiting for transfers between devices, shards(): other = lax.ppermute(blocks[:, :HALF], 'tm', swap)  1.33 us
    pallas_call x1, Pallas kernels, filter_rows(): pl.pallas_call(filter_kernel, out_shape=jax.ShapeDtypeStruct((rows, width...  1.09 us
  transfers between devices with their start and end apart: 2, of which 2 were waited for; matrix products, arithmetic and copies ran while one was open for 0% of the time, Pallas kernels for 3%

profile of v5, /device:TPU:0, one launch (start us, length us, event | category | flops | bytes accessed | tf_op | source)
XLA Modules:
  0.0 35.7 jit_solution(11882301741824164658)
XLA Ops:
  0.0 0.0 copy-start.1
  0.0 0.0 copy-start
  0.0 1.9 %shard_map.38.refs_0_ = f32[48,512]{1,0:T(8,128)S(1)} custom-call(s32[16]{0:T(128)} %index_hbm.1, f32[65]{0:T(128)} %taps_hbm.1, f32[384,512]{1,0:T(8,128)} %rec_hbm.1), custom_call_target="tpu_custom_call" | custom-call | flops 402653184 | bytes 786432 | tf_op jit(solution)/shard_map/pallas_call | solution.py:97
  1.9 3.0 %collective-permute-start = (f32[48,512]{1,0:T(8,128)S(1)}, f32[48,512]{1,0:T(8,128)S(1)}, u32[]{:S(2)}, u32[]{:S(2)}) collective-permute-start(f32[48,512]{1,0:T(8,128)S(1)} %shard_map.38.refs_0_), channel_id=1, source_target_pairs={{0,1},{1,0},{2,3},{3,2},{4,5},{5,4},{6,7},{7,6},{8,9},{9,8},{10,11... | collective-permute-start | bytes 294920 | tf_op jit(solution)/shard_map/ppermute | solution.py:292
  4.9 0.0 copy-done.1
  4.9 0.0 copy-done
  4.9 1.1 %shard_map.37.filt_ref = f32[384,512]{1,0:T(8,128)S(1)} custom-call(f32[65]{0:T(128)S(1)} %copy-done.1, f32[384,512]{1,0:T(8,128)S(1)} %copy-done), custom_call_target="tpu_custom_call" | custom-call | flops 301989888 | bytes 1572864 | tf_op jit(solution)/shard_map/pallas_call | solution.py:126
  6.0 1.7 %collective-permute-done.refs_1_ = f32[48,512]{1,0:T(8,128)S(1)} collective-permute-done((f32[48,512]{1,0:T(8,128)S(1)}, f32[48,512]{1,0:T(8,128)S(1)}, u32[]{:S(2)}, u32[]{:S(2)}) %collective-permute-start) | collective-permute-done | bytes 98336 | tf_op jit(solution)/shard_map/ppermute | solution.py:292
  7.7 0.1 shard_map.39
  7.8 20.5 %all_to_all.5.x_ref = bf16[16,32,512]{2,1,0:T(8,128)(2,1)S(1)} all-to-all(bf16[16,32,512]{2,1,0:T(8,128)(2,1)S(1)} %shard_map.39), channel_id=1, replica_groups=mesh['tm'=16,'sec'=2] {'tm'}, dimensions={0} | all-to-all | bytes 1048576 | tf_op jit(solution)/shard_map/all_to_all | solution.py:301
  28.2 0.1 collective-permute-start.1
  28.3 1.3 %collective-permute-done.1.other_ref = bf16[16,8,512]{2,1,0:T(8,128)(2,1)S(1)} collective-permute-done((bf16[16,8,512]{2,1,0:T(8,128)(2,1)S(1)}, bf16[16,8,512]{2,1,0:T(8,128)(2,1)S(1)}, u32[]{:S(2)}, u32[]{:S(2)}) %collective-permute-start.1) | collective-permute-done | bytes 131104 | tf_op jit(solution)/shard_map/ppermute | solution.py:303
  29.7 6.0 %shard_map.40 = f32[24,16,513]{2,1,0:T(8,128)} custom-call(bf16[16,32,512]{2,1,0:T(8,128)(2,1)S(1)} %all_to_all.5.x_ref, bf16[16,8,512]{2,1,0:T(8,128)(2,1)S(1)} %collective-permute-done.1.other_ref), custom_call_target="tpu_custom_call" | custom-call | tf_op jit(solution)/shard_map/pallas_call | solution.py:275
  (1 shorter events, 0.0 us)
Async XLA Ops:
  0.0 4.9 %copy-start.1 = (f32[65]{0:T(128)S(1)}, f32[65]{0:T(128)}, u32[]{:S(2)}) copy-start(f32[65]{0:T(128)} %taps_hbm.1) | copy-start | bytes 784
  0.0 4.9 %copy-start = (f32[384,512]{1,0:T(8,128)S(1)}, f32[384,512]{1,0:T(8,128)}, u32[]{:S(2)}) copy-start(f32[384,512]{1,0:T(8,128)} %rec_hbm.1) | copy-start | bytes 2359300
  1.9 5.8 %collective-permute-start = (f32[48,512]{1,0:T(8,128)S(1)}, f32[48,512]{1,0:T(8,128)S(1)}, u32[]{:S(2)}, u32[]{:S(2)}) collective-permute-start(f32[48,512]{1,0:T(8,128)S(1)} %shard_map.38.refs_0_), channel_id=1, source_target_pairs={{0,1},{1,0},{2,3},{3,2},{4,5},{5,4},{6,7},{7,6},{8,9},{9,8},{10,11... | collective-permute-start | bytes 294920 | tf_op jit(solution)/shard_map/ppermute | solution.py:292
  28.2 1.4 %collective-permute-start.1 = (bf16[16,8,512]{2,1,0:T(8,128)(2,1)S(1)}, bf16[16,8,512]{2,1,0:T(8,128)(2,1)S(1)}, u32[]{:S(2)}, u32[]{:S(2)}) collective-permute-start(bf16[16,8,512]{2,1,0:T(8,128)(2,1)S(1)} %slice.4), channel_id=1, source_target_pairs={{0,2},{2,0},{4,6},{6,4},{8,10},{10,8},{12,14},{14,12},{16,18},{18,... | collective-permute-start | bytes 393224 | tf_op jit(solution)/shard_map/ppermute | solution.py:303

commit v6 on v5

--- a/solution.py
+++ b/solution.py
@@ -53,62 +53,73 @@
     return big[:128] + (big[128:] + small)
 
 
-def share_kernel(
-    index_hbm, taps_hbm, rec_hbm, exch_ref, index_ref, taps_ref, rec_ref, hi_ref, lo_ref, ext_ref, sems, *, pair
-):
+def share_kernel(index_hbm, taps_hbm, rec_hbm, exch_ref, index_ref, taps_ref, rec_ref, sems, *, pair):
     rows, width = rec_ref.shape
     sources = index_ref.shape[0]
+    taps = taps_ref.shape[0]
     step = rows // FETCHES
-    fetches = [pltpu.make_async_copy(taps_hbm, taps_ref, sems.at[FETCHES + 1])]
+    fetches = [
+        pltpu.make_async_copy(taps_hbm, taps_ref, sems.at[FETCHES + 1]),
+        pltpu.make_async_copy(index_hbm, index_ref, sems.at[FETCHES]),
+    ]
     for i in range(FETCHES):
         part = pl.ds(i * step, step)
         fetches.append(pltpu.make_async_copy(rec_hbm.at[part, :], rec_ref.at[part, :], sems.at[i]))
-    fetches.append(pltpu.make_async_copy(index_hbm, index_ref, sems.at[FETCHES]))
     for fetch in fetches:
         fetch.start()
-    clear_edges((hi_ref, lo_ref), rows)
+    fetches[1].wait()
+    first = lax.axis_index("sec") * rows + HALO
+    at = lax.broadcasted_iota(jnp.int32, (sources, rows), 0)
+    tap = jnp.zeros((sources, rows), jnp.int32)
+    for s in range(sources):
+        tap = jnp.where(at == s, index_ref[s] - first, tap)
+    tap = lax.broadcasted_iota(jnp.int32, (sources, rows), 1) - tap
+    ring = rows + 128
+    lane = lax.broadcasted_iota(jnp.int32, (8, ring), 1)
+    base = jnp.zeros((8, ring), f32)
+    pick = jnp.zeros((sources, rows), f32)
     fetches[0].wait()
-    band = band_halves(taps_ref, 0)
+    for m in range(taps):
+        value = taps_ref[m] * SCALE
+        base = jnp.where(lane == m, value, base)
+        pick = jnp.where(tap == m, value, pick)
+    tall = jnp.concatenate([base] * (HALO // 8), axis=0)
+    down = pltpu.roll(tall, ring - 64, 1, stride=1, stride_axis=0)[:, :rows]
+    up = pltpu.roll(tall, rows - HALO, 1, stride=1, stride_axis=0)[:, :rows]
+    edges = [jnp.where(lax.axis_index("sec") == 0, up, down)] if pair else [down, up]
+    pick = jnp.concatenate([pick] + edges, axis=0)
+    count = pick.shape[0]
+    pick_hi = pick.astype(bf16)
+    both = jnp.concatenate([pick_hi, (pick - pick_hi.astype(f32)).astype(bf16)], axis=0)
+    total = jnp.zeros((count, width), f32)
     for i in range(FETCHES):
-        fetches[1 + i].wait()
-        split_rows(rec_ref[i * step : (i + 1) * step, :], hi_ref, lo_ref, 64 + i * step)
-    fetches[1 + FETCHES].wait()
-    for i in range(ext_ref.shape[0] // 128):
-        ext_ref[128 * i : 128 * i + 128, :] = band_product(band, hi_ref, lo_ref, i)
-    first = lax.axis_index("sec") * rows - HALO
-    for s in range(sources):
-        row = index_ref[s] - first
-        inside = jnp.logical_and(row >= 0, row < rows + 2 * HALO)
-        at = jnp.where(inside, row, 0)
-        exch_ref[s : s + 1, :] = jnp.where(inside, ext_ref[pl.ds(at, 1), :], 0.0)
-    down = ext_ref[:HALO, :]
-    up = ext_ref[HALO + rows : 2 * HALO + rows, :]
-    if pair:
-        exch_ref[sources:, :] = jnp.where(lax.axis_index("sec") == 0, up, down)
-    else:
-        exch_ref[sources : sources + HALO, :] = down
-        exch_ref[sources + HALO :, :] = up
+        fetches[2 + i].wait()
+        part = slice(i * step, (i + 1) * step)
+        rec = rec_ref[part, :]
+        rec_hi = rec.astype(bf16)
+        rec_lo = (rec - rec_hi.astype(f32)).astype(bf16)
+        big = jnp.dot(both[:, part], rec_hi, preferred_element_type=f32)
+        small = jnp.dot(pick_hi[:, part], rec_lo, preferred_element_type=f32)
+        total = total + (big[:count] + (big[count:] + small))
+    exch_ref[...] = total
 
 
 def share(record, fir_taps, source_index, pair):
     rows, width = record.shape
     sources = source_index.shape[0]
-    tiles = -(-(rows + 64) // 128)
+    count = sources + HALO * (1 if pair else 2)
     return pl.pallas_call(
         functools.partial(share_kernel, pair=pair),
-        out_shape=jax.ShapeDtypeStruct((sources + HALO * (1 if pair else 2), width), f32),
+        out_shape=jax.ShapeDtypeStruct((count, width), f32),
         in_specs=[pl.BlockSpec(memory_space=pltpu.HBM)] * 3,
         scratch_shapes=[
             pltpu.SMEM(source_index.shape, jnp.int32),
             pltpu.SMEM(fir_taps.shape, f32),
             pltpu.VMEM((rows, width), f32),
-            pltpu.VMEM((128 * (tiles + 1), width), bf16),
-            pltpu.VMEM((128 * (tiles + 1), width), bf16),
-            pltpu.VMEM((128 * tiles, width), f32),
             pltpu.SemaphoreType.DMA((FETCHES + 2,)),
         ],
-        compiler_params=pltpu.CompilerParams(vmem_limit_bytes=24*1024*1024),
-        cost_estimate=pl.CostEstimate(flops=2 * 3 * 128 * tiles * 256 * width, bytes_accessed=4 * rows * width, transcendentals=0),
+        compiler_params=pltpu.CompilerParams(vmem_limit_bytes=24 * 1024 * 1024),
+        cost_estimate=pl.CostEstimate(flops=6 * count * rows * width, bytes_accessed=4 * rows * width, transcendentals=0),
     )(source_index, fir_taps, record)
 
 

time: 35.9 us -> 35.4 us (0.986)
  Pallas kernels: 9.04 us -> 8.61 us
    pallas_call x1, Pallas kernels: 1.86 us -> 1.42 us  [share(): pl.pallas_call(functools.partial(share_kernel, pair=pair), out_shape=jax....]
where the time goes in v6:
time: 35.4 us; the launch traced here: 35.3 us
  blocking collectives  20.5 us (58%)
  Pallas kernels  8.61 us (24%)
  starting transfers between devices  3.11 us (9%)
  waiting for transfers between devices  3.02 us (9%)
    all_to_all x1, blocking collectives, shards(): blocks = lax.all_to_all(blocks, 'tm', 0, 0, tiled=True)  20.5 us
    pallas_call x1, Pallas kernels, correlate(): pl.pallas_call(functools.partial(corr_kernel, kc=kc, count=count), out_sh...  6.04 us
    ppermute x1, starting transfers between devices, shards(): others = (exch, lax.ppermute(exch, 'sec', [(0, 1), (1, 0)]))  3.03 us
    ppermute x1, waiting for transfers between devices, shards(): others = (exch, lax.ppermute(exch, 'sec', [(0, 1), (1, 0)]))  1.69 us
    pallas_call x1, Pallas kernels, share(): pl.pallas_call(functools.partial(share_kernel, pair=pair), out_shape=jax....  1.42 us
    ppermute x1, waiting for transfers between devices, shards(): other = lax.ppermute(blocks[:, :HALF], 'tm', swap)  1.33 us
    pallas_call x1, Pallas kernels, filter_rows(): pl.pallas_call(filter_kernel, out_shape=jax.ShapeDtypeStruct((rows, width...  1.09 us
  transfers between devices with their start and end apart: 2, of which 2 were waited for; matrix products, arithmetic and copies ran while one was open for 0% of the time, Pallas kernels for 3%

profile of v6, /device:TPU:0, one launch (start us, length us, event | category | flops | bytes accessed | tf_op | source)
XLA Modules:
  0.0 35.3 jit_solution(17430613255782582882)
XLA Ops:
  0.0 0.0 copy-start.1
  0.0 0.0 copy-start
  0.0 1.4 %shard_map.38.refs_0_ = f32[48,512]{1,0:T(8,128)S(1)} custom-call(s32[16]{0:T(128)} %index_hbm.1, f32[65]{0:T(128)} %taps_hbm.1, f32[384,512]{1,0:T(8,128)} %rec_hbm.1), custom_call_target="tpu_custom_call" | custom-call | flops 56623104 | bytes 786432 | tf_op jit(solution)/shard_map/pallas_call | solution.py:111
  1.4 3.0 %collective-permute-start = (f32[48,512]{1,0:T(8,128)S(1)}, f32[48,512]{1,0:T(8,128)S(1)}, u32[]{:S(2)}, u32[]{:S(2)}) collective-permute-start(f32[48,512]{1,0:T(8,128)S(1)} %shard_map.38.refs_0_), channel_id=1, source_target_pairs={{0,1},{1,0},{2,3},{3,2},{4,5},{5,4},{6,7},{7,6},{8,9},{9,8},{10,11... | collective-permute-start | bytes 294920 | tf_op jit(solution)/shard_map/ppermute | solution.py:303
  4.5 0.0 copy-done.1
  4.5 0.0 copy-done
  4.5 1.1 %shard_map.37.filt_ref = f32[384,512]{1,0:T(8,128)S(1)} custom-call(f32[65]{0:T(128)S(1)} %copy-done.1, f32[384,512]{1,0:T(8,128)S(1)} %copy-done), custom_call_target="tpu_custom_call" | custom-call | flops 301989888 | bytes 1572864 | tf_op jit(solution)/shard_map/pallas_call | solution.py:137
  5.6 1.7 %collective-permute-done.refs_1_ = f32[48,512]{1,0:T(8,128)S(1)} collective-permute-done((f32[48,512]{1,0:T(8,128)S(1)}, f32[48,512]{1,0:T(8,128)S(1)}, u32[]{:S(2)}, u32[]{:S(2)}) %collective-permute-start) | collective-permute-done | bytes 98336 | tf_op jit(solution)/shard_map/ppermute | solution.py:303
  7.3 0.1 shard_map.39
  7.3 20.5 %all_to_all.5.x_ref = bf16[16,32,512]{2,1,0:T(8,128)(2,1)S(1)} all-to-all(bf16[16,32,512]{2,1,0:T(8,128)(2,1)S(1)} %shard_map.39), channel_id=1, replica_groups=mesh['tm'=16,'sec'=2] {'tm'}, dimensions={0} | all-to-all | bytes 1048576 | tf_op jit(solution)/shard_map/all_to_all | solution.py:312
  27.8 0.1 collective-permute-start.1
  27.9 1.3 %collective-permute-done.1.other_ref = bf16[16,8,512]{2,1,0:T(8,128)(2,1)S(1)} collective-permute-done((bf16[16,8,512]{2,1,0:T(8,128)(2,1)S(1)}, bf16[16,8,512]{2,1,0:T(8,128)(2,1)S(1)}, u32[]{:S(2)}, u32[]{:S(2)}) %collective-permute-start.1) | collective-permute-done | bytes 131104 | tf_op jit(solution)/shard_map/ppermute | solution.py:314
  29.2 6.0 %shard_map.40 = f32[24,16,513]{2,1,0:T(8,128)} custom-call(bf16[16,32,512]{2,1,0:T(8,128)(2,1)S(1)} %all_to_all.5.x_ref, bf16[16,8,512]{2,1,0:T(8,128)(2,1)S(1)} %collective-permute-done.1.other_ref), custom_call_target="tpu_custom_call" | custom-call | tf_op jit(solution)/shard_map/pallas_call | solution.py:286
  (1 shorter events, 0.0 us)
Async XLA Ops:
  0.0 4.5 %copy-start.1 = (f32[65]{0:T(128)S(1)}, f32[65]{0:T(128)}, u32[]{:S(2)}) copy-start(f32[65]{0:T(128)} %taps_hbm.1) | copy-start | bytes 784
  0.0 4.5 %copy-start = (f32[384,512]{1,0:T(8,128)S(1)}, f32[384,512]{1,0:T(8,128)}, u32[]{:S(2)}) copy-start(f32[384,512]{1,0:T(8,128)} %rec_hbm.1) | copy-start | bytes 2359300
  1.4 5.8 %collective-permute-start = (f32[48,512]{1,0:T(8,128)S(1)}, f32[48,512]{1,0:T(8,128)S(1)}, u32[]{:S(2)}, u32[]{:S(2)}) collective-permute-start(f32[48,512]{1,0:T(8,128)S(1)} %shard_map.38.refs_0_), channel_id=1, source_target_pairs={{0,1},{1,0},{2,3},{3,2},{4,5},{5,4},{6,7},{7,6},{8,9},{9,8},{10,11... | collective-permute-start | bytes 294920 | tf_op jit(solution)/shard_map/ppermute | solution.py:303
  27.8 1.4 %collective-permute-start.1 = (bf16[16,8,512]{2,1,0:T(8,128)(2,1)S(1)}, bf16[16,8,512]{2,1,0:T(8,128)(2,1)S(1)}, u32[]{:S(2)}, u32[]{:S(2)}) collective-permute-start(bf16[16,8,512]{2,1,0:T(8,128)(2,1)S(1)} %slice.4), channel_id=1, source_target_pairs={{0,2},{2,0},{4,6},{6,4},{8,10},{10,8},{12,14},{14,12},{16,18},{18,... | collective-permute-start | bytes 393224 | tf_op jit(solution)/shard_map/ppermute | solution.py:314

commit v7 on v6

--- a/solution.py
+++ b/solution.py
@@ -17,7 +17,7 @@
 G = 32
 HALO = 32
 HALF = 8
-SENT = 4
+SENT = 2
 FETCHES = 3
 
 
@@ -264,8 +264,9 @@
         parts=[]
         for h in range(2):
             even,odd=lags(h,c),lags(h,c+1)
-            parts.append(jnp.where(wide,even,pltpu.roll(odd,64,1)))
-            parts.append(jnp.where(wide,pltpu.roll(even,64,1),odd))
+            crossed=pltpu.roll(jnp.where(wide,odd,even),64,1)
+            parts.append(jnp.where(wide,even,crossed))
+            parts.append(jnp.where(wide,crossed,odd))
         turned=jnp.concatenate(parts,axis=0).T
         for m in range(2):
             scl=esb*jnp.broadcast_to(ue[c+m:c+m+1],(16,128))
@@ -279,10 +280,11 @@
         copy.wait()
 
 
-def correlate(x,other,kc=2816):
+def correlate(x,other):
     wins,rows,win=x.shape
     count=rows-HALF
     T=wins*win
+    kc=T+256
     out=pl.pallas_call(functools.partial(corr_kernel,kc=kc,count=count),
         out_shape=jax.ShapeDtypeStruct((count,16,NLAG),f32),
         out_specs=pl.BlockSpec(memory_space=pltpu.HBM),

time: 35.4 us -> 35.1 us (level)
  no operation moved by 1% of the time
where the time goes in v7:
time: 35.1 us; the launch traced here: 34.9 us
  blocking collectives  20.5 us (58%)
  Pallas kernels  8.27 us (24%)
  starting transfers between devices  3.11 us (9%)
  waiting for transfers between devices  3.02 us (9%)
    all_to_all x1, blocking collectives, shards(): blocks = lax.all_to_all(blocks, 'tm', 0, 0, tiled=True)  20.5 us
    pallas_call x1, Pallas kernels, correlate(): pl.pallas_call(functools.partial(corr_kernel, kc=kc, count=count), out_sh...  5.7 us
    ppermute x1, starting transfers between devices, shards(): others = (exch, lax.ppermute(exch, 'sec', [(0, 1), (1, 0)]))  3.03 us
    ppermute x1, waiting for transfers between devices, shards(): others = (exch, lax.ppermute(exch, 'sec', [(0, 1), (1, 0)]))  1.69 us
    pallas_call x1, Pallas kernels, share(): pl.pallas_call(functools.partial(share_kernel, pair=pair), out_shape=jax....  1.42 us
    ppermute x1, waiting for transfers between devices, shards(): other = lax.ppermute(blocks[:, :HALF], 'tm', swap)  1.33 us
    pallas_call x1, Pallas kernels, filter_rows(): pl.pallas_call(filter_kernel, out_shape=jax.ShapeDtypeStruct((rows, width...  1.09 us
  transfers between devices with their start and end apart: 2, of which 2 were waited for; matrix products, arithmetic and copies ran while one was open for 0% of the time, Pallas kernels for 3%

profile of v7, /device:TPU:0, one launch (start us, length us, event | category | flops | bytes accessed | tf_op | source)
XLA Modules:
  0.0 34.9 jit_solution(17623016791074911514)
XLA Ops:
  0.0 0.0 copy-start.1
  0.0 0.0 copy-start
  0.0 1.4 %shard_map.38.refs_0_ = f32[48,512]{1,0:T(8,128)S(1)} custom-call(s32[16]{0:T(128)} %index_hbm.1, f32[65]{0:T(128)} %taps_hbm.1, f32[384,512]{1,0:T(8,128)} %rec_hbm.1), custom_call_target="tpu_custom_call" | custom-call | flops 56623104 | bytes 786432 | tf_op jit(solution)/shard_map/pallas_call | solution.py:111
  1.4 3.0 %collective-permute-start = (f32[48,512]{1,0:T(8,128)S(1)}, f32[48,512]{1,0:T(8,128)S(1)}, u32[]{:S(2)}, u32[]{:S(2)}) collective-permute-start(f32[48,512]{1,0:T(8,128)S(1)} %shard_map.38.refs_0_), channel_id=1, source_target_pairs={{0,1},{1,0},{2,3},{3,2},{4,5},{5,4},{6,7},{7,6},{8,9},{9,8},{10,11... | collective-permute-start | bytes 294920 | tf_op jit(solution)/shard_map/ppermute | solution.py:305
  4.5 0.0 copy-done.1
  4.5 0.0 copy-done
  4.5 1.1 %shard_map.37.filt_ref = f32[384,512]{1,0:T(8,128)S(1)} custom-call(f32[65]{0:T(128)S(1)} %copy-done.1, f32[384,512]{1,0:T(8,128)S(1)} %copy-done), custom_call_target="tpu_custom_call" | custom-call | flops 301989888 | bytes 1572864 | tf_op jit(solution)/shard_map/pallas_call | solution.py:137
  5.6 1.7 %collective-permute-done.refs_1_ = f32[48,512]{1,0:T(8,128)S(1)} collective-permute-done((f32[48,512]{1,0:T(8,128)S(1)}, f32[48,512]{1,0:T(8,128)S(1)}, u32[]{:S(2)}, u32[]{:S(2)}) %collective-permute-start) | collective-permute-done | bytes 98336 | tf_op jit(solution)/shard_map/ppermute | solution.py:305
  7.3 0.1 shard_map.39
  7.3 20.5 %all_to_all.5.x_ref = bf16[16,32,512]{2,1,0:T(8,128)(2,1)S(1)} all-to-all(bf16[16,32,512]{2,1,0:T(8,128)(2,1)S(1)} %shard_map.39), channel_id=1, replica_groups=mesh['tm'=16,'sec'=2] {'tm'}, dimensions={0} | all-to-all | bytes 1048576 | tf_op jit(solution)/shard_map/all_to_all | solution.py:314
  27.8 0.1 collective-permute-start.1
  27.9 1.3 %collective-permute-done.1.other_ref = bf16[16,8,512]{2,1,0:T(8,128)(2,1)S(1)} collective-permute-done((bf16[16,8,512]{2,1,0:T(8,128)(2,1)S(1)}, bf16[16,8,512]{2,1,0:T(8,128)(2,1)S(1)}, u32[]{:S(2)}, u32[]{:S(2)}) %collective-permute-start.1) | collective-permute-done | bytes 131104 | tf_op jit(solution)/shard_map/ppermute | solution.py:316
  29.2 5.7 %shard_map.40 = f32[24,16,513]{2,1,0:T(8,128)} custom-call(bf16[16,32,512]{2,1,0:T(8,128)(2,1)S(1)} %all_to_all.5.x_ref, bf16[16,8,512]{2,1,0:T(8,128)(2,1)S(1)} %collective-permute-done.1.other_ref), custom_call_target="tpu_custom_call" | custom-call | tf_op jit(solution)/shard_map/pallas_call | solution.py:288
  (1 shorter events, 0.0 us)
Async XLA Ops:
  0.0 4.5 %copy-start.1 = (f32[65]{0:T(128)S(1)}, f32[65]{0:T(128)}, u32[]{:S(2)}) copy-start(f32[65]{0:T(128)} %taps_hbm.1) | copy-start | bytes 784
  0.0 4.5 %copy-start = (f32[384,512]{1,0:T(8,128)S(1)}, f32[384,512]{1,0:T(8,128)}, u32[]{:S(2)}) copy-start(f32[384,512]{1,0:T(8,128)} %rec_hbm.1) | copy-start | bytes 2359300
  1.4 5.8 %collective-permute-start = (f32[48,512]{1,0:T(8,128)S(1)}, f32[48,512]{1,0:T(8,128)S(1)}, u32[]{:S(2)}, u32[]{:S(2)}) collective-permute-start(f32[48,512]{1,0:T(8,128)S(1)} %shard_map.38.refs_0_), channel_id=1, source_target_pairs={{0,1},{1,0},{2,3},{3,2},{4,5},{5,4},{6,7},{7,6},{8,9},{9,8},{10,11... | collective-permute-start | bytes 294920 | tf_op jit(solution)/shard_map/ppermute | solution.py:305
  27.8 1.4 %collective-permute-start.1 = (bf16[16,8,512]{2,1,0:T(8,128)(2,1)S(1)}, bf16[16,8,512]{2,1,0:T(8,128)(2,1)S(1)}, u32[]{:S(2)}, u32[]{:S(2)}) collective-permute-start(bf16[16,8,512]{2,1,0:T(8,128)(2,1)S(1)} %slice.4), channel_id=1, source_target_pairs={{0,2},{2,0},{4,6},{6,4},{8,10},{10,8},{12,14},{14,12},{16,18},{18,... | collective-permute-start | bytes 393224 | tf_op jit(solution)/shard_map/ppermute | solution.py:316

commit v8 on v7

--- a/solution.py
+++ b/solution.py
@@ -18,6 +18,7 @@
 HALO = 32
 HALF = 8
 SENT = 2
+AHEAD = 1
 FETCHES = 3
 
 
@@ -182,35 +183,74 @@
     )(filt, *others)
 
 
-def corr_kernel(x_ref, other_ref, out_hbm, o_ref, sems, p_ref, lo_ref, v_ref, z_ref, acc_ref, *, kc, count):
+def ready_kernel(x_ref, plate_ref, lo_ref, sum_ref, v_ref, *, count):
+    wins, _, win = x_ref.shape
+    T = wins * win
+    KT = T + 256
+    per = win // 128
+    usum = jnp.zeros((count, 128), f32)
+    blank = jnp.zeros((16, 256), bf16)
+    lo_ref[:, :256] = blank
+    lo_ref[:, 256 + T :] = blank[:, :128]
+    v_ref[:, :128] = blank[:, :128]
+    v_ref[:, 256 + T :] = blank[:, :128]
+    lane8 = lax.broadcasted_iota(jnp.int32, (8, 128), 1)
+
+    def paired(a, b):
+        later = jnp.where(lane8 < 112, pltpu.roll(a, 112, 1), pltpu.roll(b, 112, 1))
+        return jnp.concatenate([a, later], axis=0).astype(bf16)
+
+    none = jnp.zeros((8, 128), f32)
+    prev = none
+    for k in range(T // 128):
+        w, q = divmod(k, per)
+        u = x_ref[w, :, q * 128 : q * 128 + 128].astype(f32)[HALF:]
+        usum = usum + u * u
+        lo_ref[:, 256 + 128 * k : 384 + 128 * k] = u[:16].astype(bf16)
+        v_ref[:, 128 + 128 * k : 256 + 128 * k] = paired(prev, u[16:])
+        prev = u[16:]
+    v_ref[:, 128 + T : 256 + T] = paired(prev, none)
+    sum_ref[...] = usum
+    w = KT + 128
+    V = v_ref[...]
+    for j in range(G // 2 + 1):
+        plate_ref[16 * j : 16 * j + 16, :] = (pltpu.roll(V, w - j, 1) if j else V)[:, :KT]
+    X = lo_ref[...]
+    for n in range(AHEAD):
+        at = 16 * (G // 2 + 1 + n)
+        plate_ref[at : at + 16, :] = pltpu.roll(X, w - (G - n), 1)[:, :KT]
+
+
+def make_ready(x):
+    wins, rows, win = x.shape
+    T = wins * win
+    return pl.pallas_call(
+        functools.partial(ready_kernel, count=rows - HALF),
+        out_shape=(
+            jax.ShapeDtypeStruct((16 * (G // 2 + 1 + AHEAD), T + 256), bf16),
+            jax.ShapeDtypeStruct((16, T + 384), bf16),
+            jax.ShapeDtypeStruct((rows - HALF, 128), f32),
+        ),
+        scratch_shapes=[pltpu.VMEM((16, T + 384), bf16)],
+        compiler_params=pltpu.CompilerParams(vmem_limit_bytes=16 * 1024 * 1024),
+        cost_estimate=pl.CostEstimate(flops=20 * 16 * T, bytes_accessed=40 * 16 * T, transcendentals=0),
+    )(x)
+
+
+def corr_kernel(x_ref, other_ref, ready_ref, lo_ref, sum_ref, out_hbm, o_ref, sems, p_ref, z_ref, acc_ref, *, kc, count):
     wins, _, win = x_ref.shape
     T=wins*win
     KT=T+256
     nt=T//128
     per=win//128
     esum=jnp.zeros((16,128),f32)
-    usum=jnp.zeros((count,128),f32)
-    zlo=jnp.zeros((16,256),bf16)
-    lo_ref[:,:256]=zlo
-    lo_ref[:,256+T:]=zlo[:,:128]
-    v_ref[:,:128]=zlo[:,:128]
-    v_ref[:,256+T:]=zlo[:,:128]
-    lane8=lax.broadcasted_iota(jnp.int32,(8,128),1)
-    def him(a,b):
-        return jnp.concatenate([a,jnp.where(lane8<112,pltpu.roll(a,112,1),pltpu.roll(b,112,1))],axis=0).astype(bf16)
-    z8=jnp.zeros((8,128),f32)
-    prev=z8
     for k in range(nt):
         w,q=divmod(k,per); s=slice(q*128,q*128+128)
-        block=x_ref[w,:,s].astype(f32)
-        p=jnp.concatenate([block[:HALF],other_ref[w,:,s].astype(f32)],axis=0)
-        u=block[HALF:]
-        esum=esum+p*p; usum=usum+u*u
+        near=x_ref[w,:,s].astype(f32)[:HALF]
+        p=jnp.concatenate([near,other_ref[w,:,s].astype(f32)],axis=0)
+        esum=esum+p*p
         p_ref[:,128*k:128*k+128]=p.astype(bf16)
-        lo_ref[:,256+128*k:384+128*k]=u[:16].astype(bf16)
-        v_ref[:,128+128*k:256+128*k]=him(prev,u[16:])
-        prev=u[16:]
-    v_ref[:,128+T:256+T]=him(prev,z8)
+    usum=sum_ref[...]
     lane=lax.broadcasted_iota(jnp.int32,(16,128),1)
     zp=jnp.zeros((16,128),bf16)
     for q in range(4): z_ref[q,:,:512]=jnp.zeros((16,512),bf16)
@@ -226,12 +266,12 @@
         state[0]=rolls; state[1]=S
     steps=-(-KT//kc)
     def chunk(t0,first):
-        X=lo_ref[:,pl.ds(t0,kc+128)]
-        V=v_ref[:,pl.ds(t0,kc+128)]
+        X=lo_ref[...]
         w=kc+128
-        rows=[(pltpu.roll(X,w-j,1) if j else X)[:,:kc] for j in range(G+1)]
-        rows+=[(pltpu.roll(V,w-j,1) if j else V)[:,:kc] for j in range(G//2)]
-        rows.append(pltpu.roll(V,w-16,1)[:,:kc])
+        tail=16*(G//2+1)
+        rows=[(pltpu.roll(X,w-j,1) if j else X)[:,:kc] for j in range(G+1-AHEAD)]
+        rows+=[ready_ref[tail+16*n:tail+16*n+16,:] for n in range(AHEAD-1,-1,-1)]
+        rows.append(ready_ref[:tail,:])
         plate=jnp.concatenate(rows,axis=0)
         rhs=jnp.concatenate([z_ref[q,:,pl.ds(t0+512-128*a,kc)] for q in range(4) for a in range(4)],axis=0)
         d=lax.dot_general(plate,rhs,(((1,),(1,)),((),())),preferred_element_type=f32)
@@ -280,7 +320,7 @@
         copy.wait()
 
 
-def correlate(x,other):
+def correlate(x,other,ready):
     wins,rows,win=x.shape
     count=rows-HALF
     T=wins*win
@@ -288,9 +328,9 @@
     out=pl.pallas_call(functools.partial(corr_kernel,kc=kc,count=count),
         out_shape=jax.ShapeDtypeStruct((count,16,NLAG),f32),
         out_specs=pl.BlockSpec(memory_space=pltpu.HBM),
-        scratch_shapes=[pltpu.VMEM((count,16,NLAG),f32),pltpu.SemaphoreType.DMA((count//SENT,)),pltpu.VMEM((16,T),bf16),pltpu.VMEM((16,T+384),bf16),pltpu.VMEM((16,T+384),bf16),pltpu.VMEM((4,16,T+768),bf16),pltpu.VMEM((2,16*(3*G//2+2),128),f32)],
-        compiler_params=pltpu.CompilerParams(vmem_limit_bytes=48*1024*1024),
-    )(x,other)
+        scratch_shapes=[pltpu.VMEM((count,16,NLAG),f32),pltpu.SemaphoreType.DMA((count//SENT,)),pltpu.VMEM((16,T),bf16),pltpu.VMEM((4,16,T+768),bf16),pltpu.VMEM((2,16*(3*G//2+2),128),f32)],
+        compiler_params=pltpu.CompilerParams(vmem_limit_bytes=36*1024*1024),
+    )(x,other,*ready)
     return out
 
 
@@ -314,7 +354,7 @@
     blocks = lax.all_to_all(blocks, "tm", 0, 0, tiled=True)
     swap = [(i, i ^ 1) for i in range(lax.axis_size("tm"))]
     other = lax.ppermute(blocks[:, :HALF], "tm", swap)
-    return correlate(blocks, other)
+    return correlate(blocks, other, make_ready(blocks))
 
 
 def solution(mesh):

time: 35.1 us -> 34.8 us (level)
  waiting for transfers between devices: 3.02 us -> 0.01 us
  local copies, waits for them, and re-layouts: 0.02 us -> 1.8 us
  Pallas kernels: 8.27 us -> 9.22 us
    unnamed x4, local copies, waits for them, and re-layouts: 0.01 us -> 1.79 us
    ppermute x1, waiting for transfers between devices: 1.69 us -> 0.01 us  [shards(): others = (exch, lax.ppermute(exch, 'sec', [(0, 1), (1, 0)]))]
    pallas_call x0 -> x1, Pallas kernels: none -> 1.4 us  [make_ready(): pl.pallas_call(functools.partial(ready_kernel, count=rows - HALF), out_sh...]
    ppermute x1, waiting for transfers between devices: 1.33 us -> 0.01 us  [shards(): other = lax.ppermute(blocks[:, :HALF], 'tm', swap)]
    pallas_call x1, Pallas kernels: 5.7 us -> 5.34 us  [correlate(): pl.pallas_call(functools.partial(corr_kernel, kc=kc, count=count), out_sh...]
  transfers between devices with their start and end apart: 2 -> 2, of which waited for: 2 -> 0; matrix products, arithmetic and copies ran while one was open for 0% -> 0% of each run, Pallas kernels for 3% -> 7%
where the time goes in v8:
time: 34.8 us; the launch traced here: 34.6 us
  blocking collectives  20.4 us (59%)
  Pallas kernels  9.22 us (26%)
  starting transfers between devices  3.11 us (9%)
  local copies, waits for them, and re-layouts  1.8 us (5%)
    all_to_all x1, blocking collectives, shards(): blocks = lax.all_to_all(blocks, 'tm', 0, 0, tiled=True)  20.4 us
    pallas_call x1, Pallas kernels, correlate(): pl.pallas_call(functools.partial(corr_kernel, kc=kc, count=count), out_sh...  5.34 us
    ppermute x1, starting transfers between devices, shards(): others = (exch, lax.ppermute(exch, 'sec', [(0, 1), (1, 0)]))  3.03 us
    unnamed x4, local copies, waits for them, and re-layouts  1.79 us
    pallas_call x1, Pallas kernels, make_ready(): pl.pallas_call(functools.partial(ready_kernel, count=rows - HALF), out_sh...  1.4 us
    pallas_call x1, Pallas kernels, share(): pl.pallas_call(functools.partial(share_kernel, pair=pair), out_shape=jax....  1.34 us
    pallas_call x1, Pallas kernels, filter_rows(): pl.pallas_call(filter_kernel, out_shape=jax.ShapeDtypeStruct((rows, width...  1.09 us
  transfers between devices with their start and end apart: 2, of which 0 were waited for; matrix products, arithmetic and copies ran while one was open for 0% of the time, Pallas kernels for 7%

profile of v8, /device:TPU:0, one launch (start us, length us, event | category | flops | bytes accessed | tf_op | source)
XLA Modules:
  0.0 34.6 jit_solution(2103295642034173488)
XLA Ops:
  0.0 1.3 %shard_map.38.refs_0_ = f32[48,512]{1,0:T(8,128)S(1)} custom-call(s32[16]{0:T(128)} %index_hbm.1, f32[65]{0:T(128)} %taps_hbm.1, f32[384,512]{1,0:T(8,128)} %rec_hbm.1), custom_call_target="tpu_custom_call" | custom-call | flops 56623104 | bytes 786432 | tf_op jit(solution)/shard_map/pallas_call | solution.py:112
  1.3 3.0 %collective-permute-start = (f32[48,512]{1,0:T(8,128)S(1)}, f32[48,512]{1,0:T(8,128)S(1)}, u32[]{:S(2)}, u32[]{:S(2)}) collective-permute-start(f32[48,512]{1,0:T(8,128)S(1)} %shard_map.38.refs_0_), channel_id=1, source_target_pairs={{0,1},{1,0},{2,3},{3,2},{4,5},{5,4},{6,7},{7,6},{8,9},{9,8},{10,11... | collective-permute-start | bytes 294920 | tf_op jit(solution)/shard_map/ppermute | solution.py:345
  4.4 0.0 copy-start
  4.4 1.1 %copy-done = f32[384,512]{1,0:T(8,128)S(1)} copy-done((f32[384,512]{1,0:T(8,128)S(1)}, f32[384,512]{1,0:T(8,128)}, u32[]{:S(2)}) %copy-start) | copy-done | bytes 786456
  5.5 0.0 copy-start.1
  5.5 0.7 %copy-done.1 = f32[65]{0:T(128)S(1)} copy-done((f32[65]{0:T(128)S(1)}, f32[65]{0:T(128)}, u32[]{:S(2)}) %copy-start.1) | copy-done | bytes 284
  6.2 1.1 %shard_map.37.filt_ref = f32[384,512]{1,0:T(8,128)S(1)} custom-call(f32[65]{0:T(128)S(1)} %copy-done.1, f32[384,512]{1,0:T(8,128)S(1)} %copy-done), custom_call_target="tpu_custom_call" | custom-call | flops 301989888 | bytes 1572864 | tf_op jit(solution)/shard_map/pallas_call | solution.py:138
  7.3 0.0 collective-permute-done.refs_1_
  7.3 0.1 shard_map.39
  7.3 20.4 %all_to_all.5.x_ref = bf16[16,32,512]{2,1,0:T(8,128)(2,1)S(1)} all-to-all(bf16[16,32,512]{2,1,0:T(8,128)(2,1)S(1)} %shard_map.39), channel_id=1, replica_groups=mesh['tm'=16,'sec'=2] {'tm'}, dimensions={0} | all-to-all | bytes 1048576 | tf_op jit(solution)/shard_map/all_to_all | solution.py:354
  27.7 0.1 collective-permute-start.1
  27.8 1.4 %shard_map.40 = (bf16[288,8448]{1,0:T(8,128)(2,1)S(1)}, bf16[16,8576]{1,0:T(8,128)(2,1)S(1)}, f32[24,128]{1,0:T(8,128)S(1)}) custom-call(bf16[16,32,512]{2,1,0:T(8,128)(2,1)S(1)} %all_to_all.5.x_ref), custom_call_target="tpu_custom_call" | custom-call | flops 2621440 | bytes 5242880 | tf_op jit(solution)/shard_map/pallas_call | solution.py:227
  29.2 0.0 collective-permute-done.1.other_ref
  29.2 5.3 %shard_map.41 = f32[24,16,513]{2,1,0:T(8,128)} custom-call(bf16[16,32,512]{2,1,0:T(8,128)(2,1)S(1)} %all_to_all.5.x_ref, bf16[16,8,512]{2,1,0:T(8,128)(2,1)S(1)} %collective-permute-done.1.other_ref, bf16[288,8448]{1,0:T(8,128)(2,1)S(1)} %get-tuple-element.8.ready_ref, bf16[16,8576]{1,0:T(8,128)(2,1)S(1)} %get-tuple-element.9.lo_ref, ...), custom_call_target="tpu_custom_call" | custom-call | tf_op jit(solution)/shard_map/pallas_call | solution.py:328
  (1 shorter events, 0.0 us)
Async XLA Ops:
  1.3 5.9 %collective-permute-start = (f32[48,512]{1,0:T(8,128)S(1)}, f32[48,512]{1,0:T(8,128)S(1)}, u32[]{:S(2)}, u32[]{:S(2)}) collective-permute-start(f32[48,512]{1,0:T(8,128)S(1)} %shard_map.38.refs_0_), channel_id=1, source_target_pairs={{0,1},{1,0},{2,3},{3,2},{4,5},{5,4},{6,7},{7,6},{8,9},{9,8},{10,11... | collective-permute-start | bytes 294920 | tf_op jit(solution)/shard_map/ppermute | solution.py:345
  4.4 1.1 %copy-start = (f32[384,512]{1,0:T(8,128)S(1)}, f32[384,512]{1,0:T(8,128)}, u32[]{:S(2)}) copy-start(f32[384,512]{1,0:T(8,128)} %rec_hbm.1) | copy-start | bytes 2359300
  5.5 0.7 %copy-start.1 = (f32[65]{0:T(128)S(1)}, f32[65]{0:T(128)}, u32[]{:S(2)}) copy-start(f32[65]{0:T(128)} %taps_hbm.1) | copy-start | bytes 784
  27.7 1.5 %collective-permute-start.1 = (bf16[16,8,512]{2,1,0:T(8,128)(2,1)S(1)}, bf16[16,8,512]{2,1,0:T(8,128)(2,1)S(1)}, u32[]{:S(2)}, u32[]{:S(2)}) collective-permute-start(bf16[16,8,512]{2,1,0:T(8,128)(2,1)S(1)} %slice.4), channel_id=1, source_target_pairs={{0,2},{2,0},{4,6},{6,4},{8,10},{10,8},{12,14},{14,12},{16,18},{18,... | collective-permute-start | bytes 393224 | tf_op jit(solution)/shard_map/ppermute | solution.py:356

commit v9 on v8

--- a/solution.py
+++ b/solution.py
@@ -18,7 +18,6 @@
 HALO = 32
 HALF = 8
 SENT = 2
-AHEAD = 1
 FETCHES = 3
 
 
@@ -215,10 +214,6 @@
     V = v_ref[...]
     for j in range(G // 2 + 1):
         plate_ref[16 * j : 16 * j + 16, :] = (pltpu.roll(V, w - j, 1) if j else V)[:, :KT]
-    X = lo_ref[...]
-    for n in range(AHEAD):
-        at = 16 * (G // 2 + 1 + n)
-        plate_ref[at : at + 16, :] = pltpu.roll(X, w - (G - n), 1)[:, :KT]
 
 
 def make_ready(x):
@@ -227,7 +222,7 @@
     return pl.pallas_call(
         functools.partial(ready_kernel, count=rows - HALF),
         out_shape=(
-            jax.ShapeDtypeStruct((16 * (G // 2 + 1 + AHEAD), T + 256), bf16),
+            jax.ShapeDtypeStruct((16 * (G // 2 + 1), T + 256), bf16),
             jax.ShapeDtypeStruct((16, T + 384), bf16),
             jax.ShapeDtypeStruct((rows - HALF, 128), f32),
         ),
@@ -268,10 +263,8 @@
     def chunk(t0,first):
         X=lo_ref[...]
         w=kc+128
-        tail=16*(G//2+1)
-        rows=[(pltpu.roll(X,w-j,1) if j else X)[:,:kc] for j in range(G+1-AHEAD)]
-        rows+=[ready_ref[tail+16*n:tail+16*n+16,:] for n in range(AHEAD-1,-1,-1)]
-        rows.append(ready_ref[:tail,:])
+        rows=[(pltpu.roll(X,w-j,1) if j else X)[:,:kc] for j in range(G+1)]
+        rows.append(ready_ref[...])
         plate=jnp.concatenate(rows,axis=0)
         rhs=jnp.concatenate([z_ref[q,:,pl.ds(t0+512-128*a,kc)] for q in range(4) for a in range(4)],axis=0)
         d=lax.dot_general(plate,rhs,(((1,),(1,)),((),())),preferred_element_type=f32)

time: 34.8 us -> 34.8 us (level)
  no operation moved by 1% of the time
where the time goes in v9:
time: 34.8 us; the launch traced here: 34.5 us
  blocking collectives  20.4 us (59%)
  Pallas kernels  9.17 us (26%)
  starting transfers between devices  3.11 us (9%)
  local copies, waits for them, and re-layouts  1.8 us (5%)
    all_to_all x1, blocking collectives, shards(): blocks = lax.all_to_all(blocks, 'tm', 0, 0, tiled=True)  20.4 us
    pallas_call x1, Pallas kernels, correlate(): pl.pallas_call(functools.partial(corr_kernel, kc=kc, count=count), out_sh...  5.36 us
    ppermute x1, starting transfers between devices, shards(): others = (exch, lax.ppermute(exch, 'sec', [(0, 1), (1, 0)]))  3.03 us
    unnamed x4, local copies, waits for them, and re-layouts  1.79 us
    pallas_call x1, Pallas kernels, share(): pl.pallas_call(functools.partial(share_kernel, pair=pair), out_shape=jax....  1.34 us
    pallas_call x1, Pallas kernels, make_ready(): pl.pallas_call(functools.partial(ready_kernel, count=rows - HALF), out_sh...  1.33 us
    pallas_call x1, Pallas kernels, filter_rows(): pl.pallas_call(filter_kernel, out_shape=jax.ShapeDtypeStruct((rows, width...  1.09 us
  transfers between devices with their start and end apart: 2, of which 0 were waited for; matrix products, arithmetic and copies ran while one was open for 0% of the time, Pallas kernels for 7%

profile of v9, /device:TPU:0, one launch (start us, length us, event | category | flops | bytes accessed | tf_op | source)
XLA Modules:
  0.0 34.5 jit_solution(16193535200795900628)
XLA Ops:
  0.0 1.3 %shard_map.38.refs_0_ = f32[48,512]{1,0:T(8,128)S(1)} custom-call(s32[16]{0:T(128)} %index_hbm.1, f32[65]{0:T(128)} %taps_hbm.1, f32[384,512]{1,0:T(8,128)} %rec_hbm.1), custom_call_target="tpu_custom_call" | custom-call | flops 56623104 | bytes 786432 | tf_op jit(solution)/shard_map/pallas_call | solution.py:111
  1.3 3.0 %collective-permute-start = (f32[48,512]{1,0:T(8,128)S(1)}, f32[48,512]{1,0:T(8,128)S(1)}, u32[]{:S(2)}, u32[]{:S(2)}) collective-permute-start(f32[48,512]{1,0:T(8,128)S(1)} %shard_map.38.refs_0_), channel_id=1, source_target_pairs={{0,1},{1,0},{2,3},{3,2},{4,5},{5,4},{6,7},{7,6},{8,9},{9,8},{10,11... | collective-permute-start | bytes 294920 | tf_op jit(solution)/shard_map/ppermute | solution.py:338
  4.4 0.0 copy-start
  4.4 1.1 %copy-done = f32[384,512]{1,0:T(8,128)S(1)} copy-done((f32[384,512]{1,0:T(8,128)S(1)}, f32[384,512]{1,0:T(8,128)}, u32[]{:S(2)}) %copy-start) | copy-done | bytes 786456
  5.5 0.0 copy-start.1
  5.5 0.7 %copy-done.1 = f32[65]{0:T(128)S(1)} copy-done((f32[65]{0:T(128)S(1)}, f32[65]{0:T(128)}, u32[]{:S(2)}) %copy-start.1) | copy-done | bytes 284
  6.2 1.1 %shard_map.37.filt_ref = f32[384,512]{1,0:T(8,128)S(1)} custom-call(f32[65]{0:T(128)S(1)} %copy-done.1, f32[384,512]{1,0:T(8,128)S(1)} %copy-done), custom_call_target="tpu_custom_call" | custom-call | flops 301989888 | bytes 1572864 | tf_op jit(solution)/shard_map/pallas_call | solution.py:137
  7.3 0.0 collective-permute-done.refs_1_
  7.3 0.1 shard_map.39
  7.3 20.4 %all_to_all.5.x_ref = bf16[16,32,512]{2,1,0:T(8,128)(2,1)S(1)} all-to-all(bf16[16,32,512]{2,1,0:T(8,128)(2,1)S(1)} %shard_map.39), channel_id=1, replica_groups=mesh['tm'=16,'sec'=2] {'tm'}, dimensions={0} | all-to-all | bytes 1048576 | tf_op jit(solution)/shard_map/all_to_all | solution.py:347
  27.7 0.1 collective-permute-start.1
  27.8 1.3 %shard_map.40 = (bf16[272,8448]{1,0:T(8,128)(2,1)S(1)}, bf16[16,8576]{1,0:T(8,128)(2,1)S(1)}, f32[24,128]{1,0:T(8,128)S(1)}) custom-call(bf16[16,32,512]{2,1,0:T(8,128)(2,1)S(1)} %all_to_all.5.x_ref), custom_call_target="tpu_custom_call" | custom-call | flops 2621440 | bytes 5242880 | tf_op jit(solution)/shard_map/pallas_call | solution.py:222
  29.1 0.0 collective-permute-done.1.other_ref
  29.2 5.4 %shard_map.41 = f32[24,16,513]{2,1,0:T(8,128)} custom-call(bf16[16,32,512]{2,1,0:T(8,128)(2,1)S(1)} %all_to_all.5.x_ref, bf16[16,8,512]{2,1,0:T(8,128)(2,1)S(1)} %collective-permute-done.1.other_ref, bf16[272,8448]{1,0:T(8,128)(2,1)S(1)} %get-tuple-element.8.ready_ref, bf16[16,8576]{1,0:T(8,128)(2,1)S(1)} %get-tuple-element.9.lo_ref, ...), custom_call_target="tpu_custom_call" | custom-call | tf_op jit(solution)/shard_map/pallas_call | solution.py:321
  (1 shorter events, 0.0 us)
Async XLA Ops:
  1.3 5.9 %collective-permute-start = (f32[48,512]{1,0:T(8,128)S(1)}, f32[48,512]{1,0:T(8,128)S(1)}, u32[]{:S(2)}, u32[]{:S(2)}) collective-permute-start(f32[48,512]{1,0:T(8,128)S(1)} %shard_map.38.refs_0_), channel_id=1, source_target_pairs={{0,1},{1,0},{2,3},{3,2},{4,5},{5,4},{6,7},{7,6},{8,9},{9,8},{10,11... | collective-permute-start | bytes 294920 | tf_op jit(solution)/shard_map/ppermute | solution.py:338
  4.4 1.1 %copy-start = (f32[384,512]{1,0:T(8,128)S(1)}, f32[384,512]{1,0:T(8,128)}, u32[]{:S(2)}) copy-start(f32[384,512]{1,0:T(8,128)} %rec_hbm.1) | copy-start | bytes 2359300
  5.5 0.7 %copy-start.1 = (f32[65]{0:T(128)S(1)}, f32[65]{0:T(128)}, u32[]{:S(2)}) copy-start(f32[65]{0:T(128)} %taps_hbm.1) | copy-start | bytes 784
  27.7 1.4 %collective-permute-start.1 = (bf16[16,8,512]{2,1,0:T(8,128)(2,1)S(1)}, bf16[16,8,512]{2,1,0:T(8,128)(2,1)S(1)}, u32[]{:S(2)}, u32[]{:S(2)}) collective-permute-start(bf16[16,8,512]{2,1,0:T(8,128)(2,1)S(1)} %slice.4), channel_id=1, source_target_pairs={{0,2},{2,0},{4,6},{6,4},{8,10},{10,8},{12,14},{14,12},{16,18},{18,... | collective-permute-start | bytes 393224 | tf_op jit(solution)/shard_map/ppermute | solution.py:349
